TPU v7x, 32 devices: a whole 2x2x4 slice. The times are simulated.
32 devices in a mesh: groups: 2 (over y), row: 16 (over z, x, core).
Axes of the slice: x: 2, y: 2, z: 4, core: 2. Of those that a mesh axis runs over, the one named last changes fastest.
Arguments:
- activations: bfloat16 [768, 8192], P('groups', 'row'), parts along dimension 0, may hold values from -24 to 24
- norm_gain: bfloat16 [8192], P('row'), may hold values from 0.099609375 to 1.8984375
- gate_weight: bfloat16 [8192, 28672], P(None, 'row'), may hold values from -0.0625 to 0.0625
- up_weight: bfloat16 [8192, 28672], P(None, 'row'), may hold values from -0.0625 to 0.0625
- down_weight: bfloat16 [28672, 8192], P('row'), may hold values from -0.046875 to 0.046875
Outputs:
- mlp_out: bfloat16 [768, 8192], P('groups', 'row'), parts along dimension 0
There are 2 independent parts, one for each index of `groups`. A program takes and returns all parts, laid end to end along the dimension named above; an argument that names none is the same for every part. Nothing has to cross between parts.
All inputs are finite; a program needn't handle non-finite values.
Results may differ from a plain program's by a relative error of at most 0.0065.
Values may be sent and summed in bfloat16 or wider, within the bound.
No kernel may reach another device: no remote copies, remote signals or barrier semaphores. Data moves between devices by JAX's collectives and lax.ppermute only.
A program may use at most 192 MiB of HBM per device.

v0:
```python
import jax
import jax.numpy as jnp
from jax import lax
from jax.sharding import PartitionSpec as P

D = 8192


def per_device(activations, norm_gain, gate_weight, up_weight, down_weight):
    float_rows = activations.astype(jnp.float32)
    square_sums = lax.psum(jnp.sum(float_rows * float_rows, axis=1), "row")
    inv_scale = lax.rsqrt(square_sums / D + 1e-05)
    normed = (float_rows * inv_scale[:, None] * norm_gain.astype(jnp.float32)[None, :]).astype(
        jnp.bfloat16
    )
    shard_rows = lax.all_gather(normed, "row", axis=1, tiled=True)
    gate_proj = jnp.dot(shard_rows, gate_weight, preferred_element_type=jnp.float32)
    up_proj = jnp.dot(shard_rows, up_weight, preferred_element_type=jnp.float32)
    hidden = (jax.nn.silu(gate_proj) * up_proj).astype(jnp.bfloat16)
    reduced = lax.psum_scatter(
        lax.dot_general(
            down_weight, hidden, (((0,), (1,)), ((), ())), preferred_element_type=jnp.float32
        ),
        "row",
        scatter_dimension=0,
        tiled=True,
    )
    return reduced.T.astype(jnp.bfloat16)


def solution(mesh):
    in_specs = (P("groups", "row"), P("row"), P(None, "row"), P(None, "row"), P("row", None))
    out_specs = P("groups", "row")
    return jax.shard_map(
        per_device, mesh=mesh, in_specs=in_specs, out_specs=out_specs, check_vma=False
    )
```

profile of v0, /device:TPU:0, one launch (start us, length us, event | category | flops | bytes accessed | tf_op | source)
XLA Modules:
  0.0 306.2 jit_solution(5603079134771323414)
XLA Ops:
  6.5 0.0 all-gather.2.cloned.1.call-start
  6.5 0.7 convert_element_type.19
  7.2 1.2 fusion.1
  8.4 34.9 %psum.7 = f32[384]{0:T(512)S(1)} all-reduce(f32[384]{0:T(512)S(1)} %fusion.1), channel_id=1, replica_groups=mesh['groups'=2,'row'=16] {'row'}, use_global_device_ids=true, to_apply=%region_1.0 | all-reduce | flops 384 | bytes 3072 | tf_op jit(solution)/shard_map/psum | solution.py:11
  43.3 1.9 fusion.3
  45.2 0.0 all-gather.2.cloned.1.call-update
  45.2 0.0 reduce-scatter.2.cloned.1.call-start
  45.3 63.1 %all-gather.2.cloned.1.call-done = bf16[384,8192]{1,0:T(8,128)(2,1)} async-done(((bf16[384,512]{1,0:T(8,128)(2,1)}), bf16[384,8192]{1,0:T(8,128)(2,1)}) %all-gather.2.cloned.1.call-update) | async-done | bytes 6291472 | tf_op jit(solution)/shard_map/all_gather | solution.py:16
  108.3 0.0 copy-start
  108.3 19.5 %fusion.4 = f32[384,1792]{1,0:T(8,128)} fusion(bf16[384,8192]{1,0:T(8,128)(2,1)} %all-gather.2.cloned.1.call-done, bf16[8192,1792]{1,0:T(8,128)(2,1)} %param.7), kind=kOutput, calls=%fused_computation.10 | convolution fusion | flops 11274289152 | bytes 38404096 | tf_op jit(solution)/shard_map/dot_general | solution.py:17
  127.9 0.0 copy-done
  127.9 16.7 %fusion = bf16[384,1792]{1,0:T(8,128)(2,1)S(1)} fusion(bf16[384,8192]{1,0:T(8,128)(2,1)S(1)} %copy-done, bf16[8192,1792]{1,0:T(8,128)(2,1)} %param.8, f32[384,1792]{1,0:T(8,128)} %fusion.4), kind=kOutput, calls=%fused_computation.2 | convolution fusion | flops 11278417920 | bytes 39780352 | tf_op jit(solution)/shard_map/dot_general | solution.py:18
  144.6 19.8 %convolution_bitcast_fusion = f32[8192,384]{0,1:T(8,128)} fusion(bf16[384,1792]{1,0:T(8,128)(2,1)S(1)} %fusion, bf16[1792,8192]{1,0:T(8,128)(2,1)} %param.9), kind=kOutput, calls=%fused_computation | convolution fusion | flops 11274289152 | bytes 43319296 | tf_op jit(solution)/shard_map/dot_general | solution.py:21
  164.4 0.0 reduce-scatter.2.cloned.1.call-update
  164.4 133.1 %reduce-scatter.2.cloned.1.call-done = f32[512,384]{0,1:T(8,128)} async-done(((f32[8192,384]{0,1:T(8,128)}), f32[512,384]{0,1:T(8,128)}) %reduce-scatter.2.cloned.1.call-update) | async-done | bytes 786448 | tf_op jit(solution)/shard_map/reduce_scatter | solution.py:20
  297.5 1.9 convert_bitcast_fusion
  (1 shorter events, 0.0 us)
Async XLA Ops:
  6.5 101.8 %all-gather.2.cloned.1.call-start = ((), (), s32[]{:S(2)}) async-start(), calls=%async_computation.1 | async-start | bytes 6684672 | tf_op jit(solution)/shard_map/all_gather | solution.py:16
  45.2 252.3 %reduce-scatter.2.cloned.1.call-start = ((), (), s32[]{:S(2)}) async-start(), calls=%async_computation.2 | async-start | bytes 13369344 | tf_op jit(solution)/shard_map/reduce_scatter | solution.py:20
  108.3 19.6 %copy-start = (bf16[384,8192]{1,0:T(8,128)(2,1)S(1)}, bf16[384,8192]{1,0:T(8,128)(2,1)}, u32[]{:S(2)}) copy-start(bf16[384,8192]{1,0:T(8,128)(2,1)} %all-gather.2.cloned.1.call-done) | copy-start | bytes 18874372
Sparse Core Ops, SparseCore 0:
  45.3 62.9 all-gather.1
  164.5 132.9 reduce-scatter.1
where the time goes:
time: 307 us; the launch traced here: 306 us
  waiting for transfers between devices  196 us (64%)
  matrix products  56.1 us (18%)
  blocking collectives  34.9 us (11%)
  between operations  13.4 us (4%)
  other arithmetic  5.67 us (2%)
    reduce_scatter x1, waiting for transfers between devices, per_device(): lax.psum_scatter(lax.dot_general(down_weight, hidden, (((0,), (1,)), ((),...  133 us
    all_gather x1, waiting for transfers between devices, per_device(): shard_rows = lax.all_gather(normed, 'row', axis=1, tiled=True)  63.1 us
    psum x1, blocking collectives, per_device(): square_sums = lax.psum(jnp.sum(float_rows * float_rows, axis=1), 'row')  34.9 us
    dot_general x1, matrix products, per_device(): lax.dot_general(down_weight, hidden, (((0,), (1,)), ((), ())), preferred_...  19.8 us
    dot_general x1, matrix products, per_device(): jnp.dot(shard_rows, gate_weight, preferred_element_type=jnp.float32)  19.5 us
    dot_general x1, matrix products, per_device(): up_proj = jnp.dot(shard_rows, up_weight, preferred_element_type=jnp.float32)  16.7 us
  transfers between devices with their start and end apart: 2, of which 2 were waited for; matrix products, arithmetic and copies ran while one was open for 0% of the time, Pallas kernels for 0%

commit v1 on v0

v1 whole, which is shorter than its diff:
```python
import functools

import jax
import jax.numpy as jnp
from jax import lax
from jax.experimental import pallas as pl
from jax.experimental.pallas import tpu as pltpu
from jax.sharding import PartitionSpec as P

EPS = 1e-05
AXIS = "row"
VMEM_LIMIT = 40 * 1024 * 1024


def plain_per_device(features, activations, norm_gain, gate_weight, up_weight, down_weight):
    float_rows = activations.astype(jnp.float32)
    square_sums = lax.psum(jnp.sum(float_rows * float_rows, axis=1), AXIS)
    inv_scale = lax.rsqrt(square_sums / features + EPS)
    normed = (float_rows * inv_scale[:, None] * norm_gain.astype(jnp.float32)[None, :]).astype(
        jnp.bfloat16
    )
    shard_rows = lax.all_gather(normed, AXIS, axis=1, tiled=True)
    gate_proj = jnp.dot(shard_rows, gate_weight, preferred_element_type=jnp.float32)
    up_proj = jnp.dot(shard_rows, up_weight, preferred_element_type=jnp.float32)
    hidden = (jax.nn.silu(gate_proj) * up_proj).astype(jnp.bfloat16)
    reduced = lax.psum_scatter(
        lax.dot_general(
            down_weight, hidden, (((0,), (1,)), ((), ())), preferred_element_type=jnp.float32
        ),
        AXIS,
        scatter_dimension=0,
        tiled=True,
    )
    return reduced.T.astype(jnp.bfloat16)


def swap(value, mask):
    return lax.ppermute(value, AXIS, [(i, i ^ mask) for i in range(lax.axis_size(AXIS))])


def gate_up_kernel(pairs, first, last, place, inv_ref, gain_ref, *refs):
    chunks, refs = refs[: 2 * pairs], refs[2 * pairs :]
    gate_w, up_w, refs = refs[0], refs[1], refs[2:]
    if not first:
        gate_in, up_in, refs = refs[0], refs[1], refs[2:]
    if last:
        hidden_ref, gate_out, up_out, normed = refs
    else:
        gate_out, up_out, normed = refs
    step, half = pl.program_id(0), pl.program_id(1)
    width = chunks[0].shape[1]
    cols = gate_w.shape[1]
    core = place[pairs]

    for k in range(pairs):

        @pl.when((step == k) & (half == 0))
        def _(k=k):
            inv = inv_ref[:, :1]
            for which, ref in enumerate(chunks[2 * k : 2 * k + 2]):
                start = pl.multiple_of((core ^ which) * width, width)
                scaled = ref[...].astype(jnp.float32) * inv * gain_ref[k : k + 1, pl.ds(start, width)]
                normed[:, pl.ds(start, width)] = scaled.astype(jnp.bfloat16)

    where = pl.ds(pl.multiple_of(half * cols, cols), cols)
    for w_ref, src, out in (
        (gate_w, None if first else gate_in, gate_out),
        (up_w, None if first else up_in, up_out),
    ):
        product = jnp.dot(normed[...], w_ref[...], preferred_element_type=jnp.float32)

        @pl.when(step == 0)
        def _(product=product, src=src, out=out):
            if src is None:
                out[:, where] = product
            else:
                out[:, where] = src[:, where] + product

        @pl.when(step != 0)
        def _(product=product, out=out):
            out[:, where] += product

    if last:

        @pl.when(step == pairs - 1)
        def _():
            gate = gate_out[:, where]
            value = gate / (1.0 + jnp.exp(-gate)) * up_out[:, where]
            hidden_ref[:, where] = value.astype(jnp.bfloat16)


def gate_up(place, inv, gains, chunks, gate_weight, up_weight, sums, last):
    pairs = len(chunks) // 2
    tokens, width = chunks[0].shape
    units = gate_weight.shape[1]
    halves = 2
    cols = units // halves
    whole = lambda: pl.BlockSpec(memory_space=pltpu.VMEM)
    weight = lambda: pl.BlockSpec((2 * width, cols), lambda s, h, place: (place[s], h))
    first = sums is None
    acc = jax.ShapeDtypeStruct((tokens, units), jnp.float32)
    out_shape = [] if last else [acc, acc]
    scratch = [pltpu.VMEM((tokens, 2 * width), jnp.bfloat16)]
    aliases = {}
    operands = [place, inv, gains, *chunks, gate_weight, up_weight]
    in_specs = [whole() for _ in range(2 + len(chunks))] + [weight(), weight()]
    if not first:
        if not last:
            aliases = {len(operands): 0, len(operands) + 1: 1}
        operands += list(sums)
        in_specs += [whole(), whole()]
    if last:
        out_shape = [jax.ShapeDtypeStruct((tokens, units), jnp.bfloat16)]
        scratch = [pltpu.VMEM((tokens, units), jnp.float32)] * 2 + scratch
    return pl.pallas_call(
        functools.partial(gate_up_kernel, pairs, first, last),
        grid_spec=pltpu.PrefetchScalarGridSpec(
            num_scalar_prefetch=1,
            grid=(pairs, halves),
            in_specs=in_specs,
            out_specs=[whole() for _ in out_shape],
            scratch_shapes=scratch,
        ),
        out_shape=out_shape,
        input_output_aliases=aliases,
        compiler_params=pltpu.CompilerParams(vmem_limit_bytes=VMEM_LIMIT),
        cost_estimate=pl.CostEstimate(
            flops=2 * tokens * 2 * width * pairs * units * 2,
            bytes_accessed=2 * 2 * width * pairs * units * 2,
            transcendentals=0,
        ),
        name="gate_up",
    )(*operands)


def down_kernel(place, hidden_ref, w_ref, send_ref, keep_ref):
    product = jnp.dot(hidden_ref[...], w_ref[...], preferred_element_type=jnp.float32)
    step = pl.program_id(0)

    @pl.when(step % 2 == 0)
    def _():
        send_ref[0] = product.astype(jnp.bfloat16)

    @pl.when(step % 2 == 1)
    def _():
        keep_ref[0] = product


def down(place, hidden, down_weight, width):
    tokens, units = hidden.shape
    blocks = place.shape[0]
    return pl.pallas_call(
        down_kernel,
        grid_spec=pltpu.PrefetchScalarGridSpec(
            num_scalar_prefetch=1,
            grid=(blocks,),
            in_specs=[
                pl.BlockSpec(memory_space=pltpu.VMEM),
                pl.BlockSpec((units, width), lambda s, place: (0, place[s])),
            ],
            out_specs=[
                pl.BlockSpec((1, tokens, width), lambda s, place: (s // 2, 0, 0)),
                pl.BlockSpec((1, tokens, width), lambda s, place: (s // 2, 0, 0)),
            ],
        ),
        out_shape=[
            jax.ShapeDtypeStruct((blocks // 2, tokens, width), jnp.bfloat16),
            jax.ShapeDtypeStruct((blocks // 2, tokens, width), jnp.float32),
        ],
        compiler_params=pltpu.CompilerParams(vmem_limit_bytes=VMEM_LIMIT),
        cost_estimate=pl.CostEstimate(
            flops=2 * tokens * units * width * blocks,
            bytes_accessed=2 * units * width * blocks,
            transcendentals=0,
        ),
        name="down",
    )(place, hidden, down_weight)


CORE, X, Z1, Z2, Z3 = 1, 2, 4, 8, 12


def per_device(activations, norm_gain, gate_weight, up_weight, down_weight):
    tokens, width = activations.shape
    features = gate_weight.shape[0]
    me = lax.axis_index(AXIS)
    chip, core = me // 2, me % 2
    is_odd = core == 1

    own = activations
    raw = {0: own}
    raw[Z1] = swap(own, Z1)
    raw[Z3] = swap(own, Z3)
    raw[X] = swap(own, X)
    raw[Z1 | X] = swap(raw[Z1], X)
    raw[Z2] = swap(raw[Z3], Z1)
    raw[Z3 | X] = swap(raw[Z3], X)
    raw[Z2 | X] = swap(raw[Z2], X)
    for mask in (0, X, Z1, Z1 | X, Z3, Z3 | X, Z2, Z2 | X):
        raw[mask | CORE] = swap(raw[mask], CORE)

    rows = own.astype(jnp.float32)
    sums = jnp.sum(rows * rows, axis=1)
    gains = norm_gain.astype(jnp.float32)
    got = swap(jnp.concatenate([sums, gains]), CORE)
    sums = sums + got[:tokens]
    other = got[tokens:]
    gains = jnp.where(is_odd, jnp.concatenate([other, gains]), jnp.concatenate([gains, other]))
    got = swap(jnp.concatenate([sums, gains]), X)
    sums = sums + got[:tokens]
    gains = jnp.concatenate([gains, got[tokens:]])
    message = jnp.concatenate([sums, gains])
    got = {mask: swap(message, mask) for mask in (Z1, Z2, Z3)}
    sums = sums + got[Z1][:tokens] + got[Z2][:tokens] + got[Z3][:tokens]
    gain_of = {0: gains, **{mask: got[mask][tokens:] for mask in got}}
    gain_of = {m: g.reshape(2, 2 * width) for m, g in gain_of.items()}
    inv = lax.rsqrt(sums / features + EPS)
    inv = jnp.broadcast_to(inv[:, None], (tokens, 128))

    acc = None
    stages = [(0, (0, X)), (Z1, (0, X)), (Z3, (0, X)), (Z2, (0,)), (Z2, (X,))]
    for n, (plane, sides) in enumerate(stages):
        masks = [plane | side for side in sides]
        place = jnp.stack([chip ^ (m // 2) for m in masks] + [core]).astype(jnp.int32)
        gain = gain_of[plane]
        if len(sides) == 1:
            gain = gain[sides[0] // X][None]
        chunks = [raw[m | c] for m in masks for c in (0, CORE)]
        acc = gate_up(
            place, inv, gain, chunks, gate_weight, up_weight, acc, n == len(stages) - 1
        )
    hidden = acc[0]

    def plane_sum(plane):
        place = jnp.stack([me ^ (plane | m) for m in (X | CORE, X, CORE, 0)]).astype(jnp.int32)
        send, keep = down(place, hidden, down_weight, width)
        pair = keep + swap(send, CORE).astype(jnp.float32)
        there = swap(pair[0].astype(jnp.bfloat16), X)
        return pair[1] + there.astype(jnp.float32)

    far = swap(plane_sum(Z2).astype(jnp.bfloat16), Z1).astype(jnp.float32)
    far = swap((plane_sum(Z3) + far).astype(jnp.bfloat16), Z3).astype(jnp.float32)
    near = swap(plane_sum(Z1).astype(jnp.bfloat16), Z1).astype(jnp.float32)
    return (plane_sum(0) + near + far).astype(jnp.bfloat16)


def solution(mesh):
    in_specs = (P("groups", AXIS), P(AXIS), P(None, AXIS), P(None, AXIS), P(AXIS, None))
    out_specs = P("groups", AXIS)

    def body(activations, norm_gain, gate_weight, up_weight, down_weight):
        if mesh.shape[AXIS] == 16 and activations.shape[1] % 128 == 0:
            run = per_device
        else:
            run = functools.partial(plain_per_device, gate_weight.shape[0])
        return run(activations, norm_gain, gate_weight, up_weight, down_weight)

    return jax.shard_map(
        body, mesh=mesh, in_specs=in_specs, out_specs=out_specs, check_vma=False
    )
```

time: 307 us -> 175 us (0.57)
  waiting for transfers between devices: 196 us -> 63.2 us
  Pallas kernels: 0 us -> 77.5 us
  matrix products: 56.1 us -> 0 us
  blocking collectives: 34.9 us -> 0 us
  starting transfers between devices: 0.04 us -> 27 us
  between operations: 13.4 us -> 0.33 us
    reduce_scatter x1 -> x0, waiting for transfers between devices: 133 us -> none  [per_device(): lax.psum_scatter(lax.dot_general(down_weight, hidden, (((0,), (1,)), ((),...]
    pallas_call x0 -> x9, Pallas kernels: none -> 77.5 us  [the longest x5 51.3 us: gate_up(): pl.pallas_call(functools.partial(gate_up_kernel, pairs, first, last), gri...]
    ppermute x0 -> x31, waiting for transfers between devices: none -> 63.2 us  [swap(): lax.ppermute(value, AXIS, [(i, i ^ mask) for i in range(lax.axis_size(AXI...]
    all_gather x1 -> x0, waiting for transfers between devices: 63.1 us -> none  [per_device(): shard_rows = lax.all_gather(normed, 'row', axis=1, tiled=True)]
    dot_general x3 -> x0, matrix products: 56.1 us -> none  [the longest x1 19.8 us: per_device(): lax.dot_general(down_weight, hidden, (((0,), (1,)), ((), ())), preferred_...]
    psum x1 -> x0, blocking collectives: 34.9 us -> none  [per_device(): square_sums = lax.psum(jnp.sum(float_rows * float_rows, axis=1), 'row')]
    ppermute x0 -> x31, starting transfers between devices: none -> 27 us  [swap(): lax.ppermute(value, AXIS, [(i, i ^ mask) for i in range(lax.axis_size(AXI...]
  transfers between devices with their start and end apart: 2 -> 31, of which waited for: 2 -> 13; matrix products, arithmetic and copies ran while one was open for 0% -> 3% of each run, Pallas kernels for 0% -> 37%
where the time goes in v1:
time: 175 us; the launch traced here: 174 us
  Pallas kernels  77.5 us (44%)
  waiting for transfers between devices  63.2 us (36%)
  starting transfers between devices  27 us (15%)
  other arithmetic  5.1 us (3%)
    ppermute x31, waiting for transfers between devices, swap(): lax.ppermute(value, AXIS, [(i, i ^ mask) for i in range(lax.axis_size(AXI...  63.2 us
    pallas_call x5, Pallas kernels, gate_up(): pl.pallas_call(functools.partial(gate_up_kernel, pairs, first, last), gri...  51.3 us
    ppermute x31, starting transfers between devices, swap(): lax.ppermute(value, AXIS, [(i, i ^ mask) for i in range(lax.axis_size(AXI...  27 us
    pallas_call x4, Pallas kernels, down(): pl.pallas_call(down_kernel, grid_spec=pltpu.PrefetchScalarGridSpec(num_sc...  26.2 us
  transfers between devices with their start and end apart: 31, of which 13 were waited for; matrix products, arithmetic and copies ran while one was open for 3% of the time, Pallas kernels for 37%

profile of v1, /device:TPU:0, one launch (start us, length us, event | category | flops | bytes accessed | tf_op | source)
XLA Modules:
  0.0 174.4 jit_solution(4237523501175167639)
XLA Ops:
  0.0 2.9 %collective-permute-start.18 = (bf16[384,512]{1,0:T(8,128)(2,1)}, bf16[384,512]{1,0:T(8,128)(2,1)S(1)}, u32[]{:S(2)}, u32[]{:S(2)}) collective-permute-start(bf16[384,512]{1,0:T(8,128)(2,1)} %refs_0_.1), channel_id=1, source_target_pairs={{0,2},{1,3},{2,0},{3,1},{4,6},{5,7},{6,4},{7,5},{8,10},{9,11},{10,... | collective-permute-start | bytes 1179656 | tf_op jit(solution)/shard_map/ppermute | solution.py:38
  4.5 2.5 %collective-permute-start.5 = (bf16[384,512]{1,0:T(8,128)(2,1)}, bf16[384,512]{1,0:T(8,128)(2,1)S(1)}, u32[]{:S(2)}, u32[]{:S(2)}) collective-permute-start(bf16[384,512]{1,0:T(8,128)(2,1)} %refs_0_.1), channel_id=1, source_target_pairs={{0,12},{1,13},{2,14},{3,15},{4,8},{5,9},{6,10},{7,11},{8,4},{9,5},... | collective-permute-start | bytes 1179656 | tf_op jit(solution)/shard_map/ppermute | solution.py:38
  10.8 3.0 %collective-permute-done.1 = f32[1408]{0:T(1024)S(1)} collective-permute-done((f32[1408]{0:T(1024)S(1)}, f32[1408]{0:T(1024)S(1)}, u32[]{:S(2)}, u32[]{:S(2)}) %collective-permute-start.1) | collective-permute-done | bytes 5664 | tf_op jit(solution)/shard_map/ppermute | solution.py:38
  14.6 2.4 %collective-permute-start.3 = (f32[2432]{0:T(1024)S(1)}, f32[2432]{0:T(1024)S(1)}, u32[]{:S(2)}, u32[]{:S(2)}) collective-permute-start(f32[2432]{0:T(1024)S(1)} %pad_maximum_fusion), channel_id=1, source_target_pairs={{0,8},{1,9},{2,10},{3,11},{4,12},{5,13},{6,14},{7,15},{8,0},{9,1},... | collective-permute-start | bytes 29192 | tf_op jit(solution)/shard_map/ppermute | solution.py:38
  17.0 6.2 %collective-permute-done.2 = f32[2432]{0:T(1024)S(1)} collective-permute-done((f32[2432]{0:T(1024)S(1)}, f32[2432]{0:T(1024)S(1)}, u32[]{:S(2)}, u32[]{:S(2)}) %collective-permute-start.2) | collective-permute-done | bytes 9760 | tf_op jit(solution)/shard_map/ppermute | solution.py:38
  23.2 2.9 %collective-permute-start.4 = (f32[2432]{0:T(1024)S(1)}, f32[2432]{0:T(1024)S(1)}, u32[]{:S(2)}, u32[]{:S(2)}) collective-permute-start(f32[2432]{0:T(1024)S(1)} %pad_maximum_fusion), channel_id=1, source_target_pairs={{0,12},{1,13},{2,14},{3,15},{4,8},{5,9},{6,10},{7,11},{8,4},{9,5},... | collective-permute-start | bytes 29192 | tf_op jit(solution)/shard_map/ppermute | solution.py:38
  26.1 2.6 %collective-permute-done.4 = f32[2432]{0:T(1024)S(1)} collective-permute-done((f32[2432]{0:T(1024)S(1)}, f32[2432]{0:T(1024)S(1)}, u32[]{:S(2)}, u32[]{:S(2)}) %collective-permute-start.4) | collective-permute-done | bytes 9760 | tf_op jit(solution)/shard_map/ppermute | solution.py:38
  31.7 9.6 %collective-permute-done.15.refs_2_ = bf16[384,512]{1,0:T(8,128)(2,1)S(1)} collective-permute-done((bf16[384,512]{1,0:T(8,128)(2,1)S(1)}, bf16[384,512]{1,0:T(8,128)(2,1)S(1)}, u32[]{:S(2)}, u32[]{:S(2)}) %collective-permute-start.15) | collective-permute-done | bytes 393248 | tf_op jit(solution)/shard_map/ppermute | solution.py:38
  43.3 12.1 %gate_up.5 = (f32[384,1792]{1,0:T(8,128)S(1)}, f32[384,1792]{1,0:T(8,128)S(1)}) custom-call(s32[3]{0:T(128)S(1)} %add_add_fusion.2.place, f32[384,128]{1,0:T(8,128)S(1)} %broadcast_in_dim.2.inv_ref, f32[2,1024]{1,0:T(2,128)S(1)} %reshape.19.gain_ref, bf16[384,512]{1,0:T(8,128)(2,1)S(1)} %copy-done, bf16[384,512]{1,0:T(8,128)(2,1)S(1)} %collective-permute-done.17.refs_1_, ...), custom_call_target="tpu_custom_call" | custom-call | flops 5637144576 | bytes 14680064 | tf_op jit(solution)/shard_map/gate_up/pallas_call | solution.py:115
  57.3 12.9 %gate_up.6 = (f32[384,1792]{1,0:T(8,128)S(1)}, f32[384,1792]{1,0:T(8,128)S(1)}) custom-call(s32[3]{0:T(128)S(1)} %add_add_fusion.1.place, f32[384,128]{1,0:T(8,128)S(1)} %broadcast_in_dim.2.inv_ref, f32[2,1024]{1,0:T(2,128)S(1)} %reshape.18.gain_ref, ...), custom_call_target="tpu_custom_call", output_to_operand_aliasing={{0}: (9, {}), {1}: (10, {})} | custom-call | flops 5637144576 | bytes 14680064 | tf_op jit(solution)/shard_map/gate_up/pallas_call | solution.py:115
  70.2 12.9 %gate_up.7 = (f32[384,1792]{1,0:T(8,128)S(1)}, f32[384,1792]{1,0:T(8,128)S(1)}) custom-call(s32[3]{0:T(128)S(1)} %add_add_fusion.place, f32[384,128]{1,0:T(8,128)S(1)} %broadcast_in_dim.2.inv_ref, f32[2,1024]{1,0:T(2,128)S(1)} %reshape.17.gain_ref, ...), custom_call_target="tpu_custom_call", output_to_operand_aliasing={{0}: (9, {}), {1}: (10, {})} | custom-call | flops 5637144576 | bytes 14680064 | tf_op jit(solution)/shard_map/gate_up/pallas_call | solution.py:115
  83.1 6.6 %gate_up.8 = (f32[384,1792]{1,0:T(8,128)S(1)}, f32[384,1792]{1,0:T(8,128)S(1)}) custom-call(s32[2]{0:T(128)S(1)} %pad_add_fusion.2.place, f32[384,128]{1,0:T(8,128)S(1)} %broadcast_in_dim.2.inv_ref, f32[1,1024]{1,0:T(1,128)S(1)} %bitcast.66, bf16[384,512]{1,0:T(8,128)(2,1)S(1)} %collective-permute-done.6.refs_0_, ...), custom_call_target="tpu_custom_call", output_to_operand_aliasing={{0}: (7, {}), {1}: (8, {})} | custom-call | flops 2818572288 | bytes 7340032 | tf_op jit(solution)/shard_map/gate_up/pallas_call | solution.py:115
  89.8 6.8 %gate_up.9.hidden_ref = bf16[384,1792]{1,0:T(8,128)(2,1)S(1)} custom-call(s32[2]{0:T(128)S(1)} %pad_add_fusion.1.place, f32[384,128]{1,0:T(8,128)S(1)} %broadcast_in_dim.2.inv_ref, f32[1,1024]{1,0:T(1,128)S(1)} %bitcast.65, bf16[384,512]{1,0:T(8,128)(2,1)S(1)} %collective-permute-done.7.refs_0_, bf16[384,512]{1,0:T(8,128)(2,1)S(1)} %collective-permute-done.8.refs_1_, ...), custom_call_target="tpu_custom_call" | custom-call | flops 2818572288 | bytes 7340032 | tf_op jit(solution)/shard_map/gate_up/pallas_call | solution.py:115
  96.6 6.5 %down.5 = (bf16[2,384,512]{2,1,0:T(8,128)(2,1)S(1)}, f32[2,384,512]{2,1,0:T(8,128)S(1)}) custom-call(s32[4]{0:T(128)S(1)} %pad_add_fusion.3.place, bf16[384,1792]{1,0:T(8,128)(2,1)S(1)} %gate_up.9.hidden_ref, bf16[1792,8192]{1,0:T(8,128)(2,1)} %w_ref.7), custom_call_target="tpu_custom_call" | custom-call | flops 2818572288 | bytes 7340032 | tf_op jit(solution)/shard_map/down/pallas_call | solution.py:152
  103.7 6.7 %down.7 = (bf16[2,384,512]{2,1,0:T(8,128)(2,1)S(1)}, f32[2,384,512]{2,1,0:T(8,128)S(1)}) custom-call(s32[4]{0:T(128)S(1)} %pad_add_fusion.5.place, bf16[384,1792]{1,0:T(8,128)(2,1)S(1)} %gate_up.9.hidden_ref, bf16[1792,8192]{1,0:T(8,128)(2,1)} %w_ref.7), custom_call_target="tpu_custom_call" | custom-call | flops 2818572288 | bytes 7340032 | tf_op jit(solution)/shard_map/down/pallas_call | solution.py:152
  110.4 6.5 %down.6 = (bf16[2,384,512]{2,1,0:T(8,128)(2,1)S(1)}, f32[2,384,512]{2,1,0:T(8,128)S(1)}) custom-call(s32[4]{0:T(128)S(1)} %pad_add_fusion.4.place, bf16[384,1792]{1,0:T(8,128)(2,1)S(1)} %gate_up.9.hidden_ref, bf16[1792,8192]{1,0:T(8,128)(2,1)} %w_ref.7), custom_call_target="tpu_custom_call" | custom-call | flops 2818572288 | bytes 7340032 | tf_op jit(solution)/shard_map/down/pallas_call | solution.py:152
  117.5 6.5 %down.4 = (bf16[2,384,512]{2,1,0:T(8,128)(2,1)S(1)}, f32[2,384,512]{2,1,0:T(8,128)S(1)}) custom-call(s32[4]{0:T(128)S(1)} %pad_add_fusion.place, bf16[384,1792]{1,0:T(8,128)(2,1)S(1)} %gate_up.9.hidden_ref, bf16[1792,8192]{1,0:T(8,128)(2,1)} %w_ref.7), custom_call_target="tpu_custom_call" | custom-call | flops 2818572288 | bytes 7340032 | tf_op jit(solution)/shard_map/down/pallas_call | solution.py:152
  128.1 16.7 %collective-permute-done.28 = bf16[384,512]{1,0:T(8,128)(2,1)S(1)} collective-permute-done((bf16[384,512]{1,0:T(8,128)(2,1)S(1)}, bf16[384,512]{1,0:T(8,128)(2,1)S(1)}, u32[]{:S(2)}, u32[]{:S(2)}) %collective-permute-start.28) | collective-permute-done | bytes 393248 | tf_op jit(solution)/shard_map/ppermute | solution.py:38
  145.8 2.1 %collective-permute-start.24 = (bf16[384,512]{1,0:T(8,128)(2,1)S(1)}, bf16[384,512]{1,0:T(8,128)(2,1)S(1)}, u32[]{:S(2)}, u32[]{:S(2)}) collective-permute-start(bf16[384,512]{1,0:T(8,128)(2,1)S(1)} %fusion.6), channel_id=1, source_target_pairs={{0,4},{1,5},{2,6},{3,7},{4,0},{5,1},{6,2},{7,3},{8,12},{9,13},{10,... | collective-permute-start | bytes 1179656 | tf_op jit(solution)/shard_map/ppermute | solution.py:38
  147.9 5.3 %collective-permute-done.26 = bf16[384,512]{1,0:T(8,128)(2,1)S(1)} collective-permute-done((bf16[384,512]{1,0:T(8,128)(2,1)S(1)}, bf16[384,512]{1,0:T(8,128)(2,1)S(1)}, u32[]{:S(2)}, u32[]{:S(2)}) %collective-permute-start.26) | collective-permute-done | bytes 393248 | tf_op jit(solution)/shard_map/ppermute | solution.py:38
  153.2 3.8 %collective-permute-done.29 = bf16[384,512]{1,0:T(8,128)(2,1)S(1)} collective-permute-done((bf16[384,512]{1,0:T(8,128)(2,1)S(1)}, bf16[384,512]{1,0:T(8,128)(2,1)S(1)}, u32[]{:S(2)}, u32[]{:S(2)}) %collective-permute-start.29) | collective-permute-done | bytes 393248 | tf_op jit(solution)/shard_map/ppermute | solution.py:38
  157.3 2.9 %collective-permute-start.30 = (bf16[384,512]{1,0:T(8,128)(2,1)S(1)}, bf16[384,512]{1,0:T(8,128)(2,1)S(1)}, u32[]{:S(2)}, u32[]{:S(2)}) collective-permute-start(bf16[384,512]{1,0:T(8,128)(2,1)S(1)} %fusion.4), channel_id=1, source_target_pairs={{0,12},{1,13},{2,14},{3,15},{4,8},{5,9},{6,10},{7,11},{8,4},{9,5},... | collective-permute-start | bytes 1179656 | tf_op jit(solution)/shard_map/ppermute | solution.py:38
  161.3 2.8 %collective-permute-done.24 = bf16[384,512]{1,0:T(8,128)(2,1)S(1)} collective-permute-done((bf16[384,512]{1,0:T(8,128)(2,1)S(1)}, bf16[384,512]{1,0:T(8,128)(2,1)S(1)}, u32[]{:S(2)}, u32[]{:S(2)}) %collective-permute-start.24) | collective-permute-done | bytes 393248 | tf_op jit(solution)/shard_map/ppermute | solution.py:38
  164.1 9.4 %collective-permute-done.30 = bf16[384,512]{1,0:T(8,128)(2,1)S(1)} collective-permute-done((bf16[384,512]{1,0:T(8,128)(2,1)S(1)}, bf16[384,512]{1,0:T(8,128)(2,1)S(1)}, u32[]{:S(2)}, u32[]{:S(2)}) %collective-permute-start.30) | collective-permute-done | bytes 393248 | tf_op jit(solution)/shard_map/ppermute | solution.py:38
  (89 shorter events, 21.5 us)
Async XLA Ops:
  0.0 28.7 %collective-permute-start.18 = (bf16[384,512]{1,0:T(8,128)(2,1)}, bf16[384,512]{1,0:T(8,128)(2,1)S(1)}, u32[]{:S(2)}, u32[]{:S(2)}) collective-permute-start(bf16[384,512]{1,0:T(8,128)(2,1)} %refs_0_.1), channel_id=1, source_target_pairs={{0,2},{1,3},{2,0},{3,1},{4,6},{5,7},{6,4},{7,5},{8,10},{9,11},{10,... | collective-permute-start | bytes 1179656 | tf_op jit(solution)/shard_map/ppermute | solution.py:38
  2.9 26.4 %collective-permute-start.13 = (bf16[384,512]{1,0:T(8,128)(2,1)}, bf16[384,512]{1,0:T(8,128)(2,1)S(1)}, u32[]{:S(2)}, u32[]{:S(2)}) collective-permute-start(bf16[384,512]{1,0:T(8,128)(2,1)} %refs_0_.1), channel_id=1, source_target_pairs={{0,4},{1,5},{2,6},{3,7},{4,0},{5,1},{6,2},{7,3},{8,12},{9,13},{10,... | collective-permute-start | bytes 1179656 | tf_op jit(solution)/shard_map/ppermute | solution.py:38
  4.5 25.3 %collective-permute-start.5 = (bf16[384,512]{1,0:T(8,128)(2,1)}, bf16[384,512]{1,0:T(8,128)(2,1)S(1)}, u32[]{:S(2)}, u32[]{:S(2)}) collective-permute-start(bf16[384,512]{1,0:T(8,128)(2,1)} %refs_0_.1), channel_id=1, source_target_pairs={{0,12},{1,13},{2,14},{3,15},{4,8},{5,9},{6,10},{7,11},{8,4},{9,5},... | collective-permute-start | bytes 1179656 | tf_op jit(solution)/shard_map/ppermute | solution.py:38
  14.6 15.2 %collective-permute-start.3 = (f32[2432]{0:T(1024)S(1)}, f32[2432]{0:T(1024)S(1)}, u32[]{:S(2)}, u32[]{:S(2)}) collective-permute-start(f32[2432]{0:T(1024)S(1)} %pad_maximum_fusion), channel_id=1, source_target_pairs={{0,8},{1,9},{2,10},{3,11},{4,12},{5,13},{6,14},{7,15},{8,0},{9,1},... | collective-permute-start | bytes 29192 | tf_op jit(solution)/shard_map/ppermute | solution.py:38
  29.3 12.0 %collective-permute-start.15 = (bf16[384,512]{1,0:T(8,128)(2,1)S(1)}, bf16[384,512]{1,0:T(8,128)(2,1)S(1)}, u32[]{:S(2)}, u32[]{:S(2)}) collective-permute-start(bf16[384,512]{1,0:T(8,128)(2,1)S(1)} %collective-permute-done.13.refs_0_), channel_id=1, source_target_pairs={{0,2},{1,3},{2,0},{3,1},{4,6},{5,7},{6,4},{7,5},{8,10},{9,11},{10,... | collective-permute-start | bytes 1179656 | tf_op jit(solution)/shard_map/ppermute | solution.py:38
  29.9 11.4 %collective-permute-start.6 = (bf16[384,512]{1,0:T(8,128)(2,1)S(1)}, bf16[384,512]{1,0:T(8,128)(2,1)S(1)}, u32[]{:S(2)}, u32[]{:S(2)}) collective-permute-start(bf16[384,512]{1,0:T(8,128)(2,1)S(1)} %collective-permute-done.5.refs_0_), channel_id=1, source_target_pairs={{0,4},{1,5},{2,6},{3,7},{4,0},{5,1},{6,2},{7,3},{8,12},{9,13},{10,... | collective-permute-start | bytes 1179656 | tf_op jit(solution)/shard_map/ppermute | solution.py:38
  29.9 25.5 %collective-permute-start.14 = (bf16[384,512]{1,0:T(8,128)(2,1)S(1)}, bf16[384,512]{1,0:T(8,128)(2,1)S(1)}, u32[]{:S(2)}, u32[]{:S(2)}) collective-permute-start(bf16[384,512]{1,0:T(8,128)(2,1)S(1)} %collective-permute-done.13.refs_0_), channel_id=1, source_target_pairs={{0,1},{1,0},{2,3},{3,2},{4,5},{5,4},{6,7},{7,6},{8,9},{9,8},{10,11... | collective-permute-start | bytes 1179656 | tf_op jit(solution)/shard_map/ppermute | solution.py:38
  30.7 24.8 %collective-permute-start.11 = (bf16[384,512]{1,0:T(8,128)(2,1)S(1)}, bf16[384,512]{1,0:T(8,128)(2,1)S(1)}, u32[]{:S(2)}, u32[]{:S(2)}) collective-permute-start(bf16[384,512]{1,0:T(8,128)(2,1)S(1)} %collective-permute-done.5.refs_0_), channel_id=1, source_target_pairs={{0,2},{1,3},{2,0},{3,1},{4,6},{5,7},{6,4},{7,5},{8,10},{9,11},{10,... | collective-permute-start | bytes 1179656 | tf_op jit(solution)/shard_map/ppermute | solution.py:38
  31.5 38.6 %collective-permute-start.10 = (bf16[384,512]{1,0:T(8,128)(2,1)S(1)}, bf16[384,512]{1,0:T(8,128)(2,1)S(1)}, u32[]{:S(2)}, u32[]{:S(2)}) collective-permute-start(bf16[384,512]{1,0:T(8,128)(2,1)S(1)} %collective-permute-done.5.refs_0_), channel_id=1, source_target_pairs={{0,1},{1,0},{2,3},{3,2},{4,5},{5,4},{6,7},{7,6},{8,9},{9,8},{10,11... | collective-permute-start | bytes 1179656 | tf_op jit(solution)/shard_map/ppermute | solution.py:38
  41.3 16.0 %collective-permute-start.16 = (bf16[384,512]{1,0:T(8,128)(2,1)S(1)}, bf16[384,512]{1,0:T(8,128)(2,1)S(1)}, u32[]{:S(2)}, u32[]{:S(2)}) collective-permute-start(bf16[384,512]{1,0:T(8,128)(2,1)S(1)} %collective-permute-done.15.refs_2_), channel_id=1, source_target_pairs={{0,1},{1,0},{2,3},{3,2},{4,5},{5,4},{6,7},{7,6},{8,9},{9,8},{10,11... | collective-permute-start | bytes 1179656 | tf_op jit(solution)/shard_map/ppermute | solution.py:38
  41.3 16.0 %collective-permute-start.7 = (bf16[384,512]{1,0:T(8,128)(2,1)S(1)}, bf16[384,512]{1,0:T(8,128)(2,1)S(1)}, u32[]{:S(2)}, u32[]{:S(2)}) collective-permute-start(bf16[384,512]{1,0:T(8,128)(2,1)S(1)} %collective-permute-done.6.refs_0_), channel_id=1, source_target_pairs={{0,2},{1,3},{2,0},{3,1},{4,6},{5,7},{6,4},{7,5},{8,10},{9,11},{10,... | collective-permute-start | bytes 1179656 | tf_op jit(solution)/shard_map/ppermute | solution.py:38
  55.4 27.8 %collective-permute-start.9 = (bf16[384,512]{1,0:T(8,128)(2,1)S(1)}, bf16[384,512]{1,0:T(8,128)(2,1)S(1)}, u32[]{:S(2)}, u32[]{:S(2)}) collective-permute-start(bf16[384,512]{1,0:T(8,128)(2,1)S(1)} %collective-permute-done.6.refs_0_), channel_id=1, source_target_pairs={{0,1},{1,0},{2,3},{3,2},{4,5},{5,4},{6,7},{7,6},{8,9},{9,8},{10,11... | collective-permute-start | bytes 1179656 | tf_op jit(solution)/shard_map/ppermute | solution.py:38
  55.5 14.7 %collective-permute-start.12 = (bf16[384,512]{1,0:T(8,128)(2,1)S(1)}, bf16[384,512]{1,0:T(8,128)(2,1)S(1)}, u32[]{:S(2)}, u32[]{:S(2)}) collective-permute-start(bf16[384,512]{1,0:T(8,128)(2,1)S(1)} %collective-permute-done.11.refs_2_), channel_id=1, source_target_pairs={{0,1},{1,0},{2,3},{3,2},{4,5},{5,4},{6,7},{7,6},{8,9},{9,8},{10,11... | collective-permute-start | bytes 1179656 | tf_op jit(solution)/shard_map/ppermute | solution.py:38
  57.3 32.5 %collective-permute-start.8 = (bf16[384,512]{1,0:T(8,128)(2,1)S(1)}, bf16[384,512]{1,0:T(8,128)(2,1)S(1)}, u32[]{:S(2)}, u32[]{:S(2)}) collective-permute-start(bf16[384,512]{1,0:T(8,128)(2,1)S(1)} %collective-permute-done.7.refs_0_), channel_id=1, source_target_pairs={{0,1},{1,0},{2,3},{3,2},{4,5},{5,4},{6,7},{7,6},{8,9},{9,8},{10,11... | collective-permute-start | bytes 1179656 | tf_op jit(solution)/shard_map/ppermute | solution.py:38
  103.1 21.0 %collective-permute-start.22 = (bf16[2,384,512]{2,1,0:T(8,128)(2,1)S(1)}, bf16[2,384,512]{2,1,0:T(8,128)(2,1)S(1)}, u32[]{:S(2)}, u32[]{:S(2)}) collective-permute-start(bf16[2,384,512]{2,1,0:T(8,128)(2,1)S(1)} %get-tuple-element.32), channel_id=1, source_target_pairs={{0,1},{1,0},{2,3},{3,2},{4,5},{5,4},{6,7},{7,6},{8,9},{9,8},{10,11... | collective-permute-start | bytes 2359304 | tf_op jit(solution)/shard_map/ppermute | solution.py:38
  110.4 14.7 %collective-permute-start.27 = (bf16[2,384,512]{2,1,0:T(8,128)(2,1)S(1)}, bf16[2,384,512]{2,1,0:T(8,128)(2,1)S(1)}, u32[]{:S(2)}, u32[]{:S(2)}) collective-permute-start(bf16[2,384,512]{2,1,0:T(8,128)(2,1)S(1)} %get-tuple-element.36), channel_id=1, source_target_pairs={{0,1},{1,0},{2,3},{3,2},{4,5},{5,4},{6,7},{7,6},{8,9},{9,8},{10,11... | collective-permute-start | bytes 2359304 | tf_op jit(solution)/shard_map/ppermute | solution.py:38
  116.9 10.0 %collective-permute-start.25 = (bf16[2,384,512]{2,1,0:T(8,128)(2,1)S(1)}, bf16[2,384,512]{2,1,0:T(8,128)(2,1)S(1)}, u32[]{:S(2)}, u32[]{:S(2)}) collective-permute-start(bf16[2,384,512]{2,1,0:T(8,128)(2,1)S(1)} %get-tuple-element.34), channel_id=1, source_target_pairs={{0,1},{1,0},{2,3},{3,2},{4,5},{5,4},{6,7},{7,6},{8,9},{9,8},{10,11... | collective-permute-start | bytes 2359304 | tf_op jit(solution)/shard_map/ppermute | solution.py:38
  124.4 21.3 %collective-permute-start.23 = (bf16[384,512]{1,0:T(8,128)(2,1)S(1)}, bf16[384,512]{1,0:T(8,128)(2,1)S(1)}, u32[]{:S(2)}, u32[]{:S(2)}) collective-permute-start(bf16[384,512]{1,0:T(8,128)(2,1)S(1)} %fusion.12), channel_id=1, source_target_pairs={{0,2},{1,3},{2,0},{3,1},{4,6},{5,7},{6,4},{7,5},{8,10},{9,11},{10,... | collective-permute-start | bytes 1179656 | tf_op jit(solution)/shard_map/ppermute | solution.py:38
  125.3 19.5 %collective-permute-start.28 = (bf16[384,512]{1,0:T(8,128)(2,1)S(1)}, bf16[384,512]{1,0:T(8,128)(2,1)S(1)}, u32[]{:S(2)}, u32[]{:S(2)}) collective-permute-start(bf16[384,512]{1,0:T(8,128)(2,1)S(1)} %fusion.14), channel_id=1, source_target_pairs={{0,2},{1,3},{2,0},{3,1},{4,6},{5,7},{6,4},{7,5},{8,10},{9,11},{10,... | collective-permute-start | bytes 1179656 | tf_op jit(solution)/shard_map/ppermute | solution.py:38
  127.2 26.0 %collective-permute-start.26 = (bf16[384,512]{1,0:T(8,128)(2,1)S(1)}, bf16[384,512]{1,0:T(8,128)(2,1)S(1)}, u32[]{:S(2)}, u32[]{:S(2)}) collective-permute-start(bf16[384,512]{1,0:T(8,128)(2,1)S(1)} %fusion.13), channel_id=1, source_target_pairs={{0,2},{1,3},{2,0},{3,1},{4,6},{5,7},{6,4},{7,5},{8,10},{9,11},{10,... | collective-permute-start | bytes 1179656 | tf_op jit(solution)/shard_map/ppermute | solution.py:38
  145.0 12.1 %collective-permute-start.29 = (bf16[384,512]{1,0:T(8,128)(2,1)S(1)}, bf16[384,512]{1,0:T(8,128)(2,1)S(1)}, u32[]{:S(2)}, u32[]{:S(2)}) collective-permute-start(bf16[384,512]{1,0:T(8,128)(2,1)S(1)} %fusion.1), channel_id=1, source_target_pairs={{0,4},{1,5},{2,6},{3,7},{4,0},{5,1},{6,2},{7,3},{8,12},{9,13},{10,... | collective-permute-start | bytes 1179656 | tf_op jit(solution)/shard_map/ppermute | solution.py:38
  145.1 16.2 %collective-permute-start.21 = (bf16[384,512]{1,0:T(8,128)(2,1)S(1)}, bf16[384,512]{1,0:T(8,128)(2,1)S(1)}, u32[]{:S(2)}, u32[]{:S(2)}) collective-permute-start(bf16[384,512]{1,0:T(8,128)(2,1)S(1)} %fusion.11), channel_id=1, source_target_pairs={{0,2},{1,3},{2,0},{3,1},{4,6},{5,7},{6,4},{7,5},{8,10},{9,11},{10,... | collective-permute-start | bytes 1179656 | tf_op jit(solution)/shard_map/ppermute | solution.py:38
  145.8 18.2 %collective-permute-start.24 = (bf16[384,512]{1,0:T(8,128)(2,1)S(1)}, bf16[384,512]{1,0:T(8,128)(2,1)S(1)}, u32[]{:S(2)}, u32[]{:S(2)}) collective-permute-start(bf16[384,512]{1,0:T(8,128)(2,1)S(1)} %fusion.6), channel_id=1, source_target_pairs={{0,4},{1,5},{2,6},{3,7},{4,0},{5,1},{6,2},{7,3},{8,12},{9,13},{10,... | collective-permute-start | bytes 1179656 | tf_op jit(solution)/shard_map/ppermute | solution.py:38
  157.3 16.2 %collective-permute-start.30 = (bf16[384,512]{1,0:T(8,128)(2,1)S(1)}, bf16[384,512]{1,0:T(8,128)(2,1)S(1)}, u32[]{:S(2)}, u32[]{:S(2)}) collective-permute-start(bf16[384,512]{1,0:T(8,128)(2,1)S(1)} %fusion.4), channel_id=1, source_target_pairs={{0,12},{1,13},{2,14},{3,15},{4,8},{5,9},{6,10},{7,11},{8,4},{9,5},... | collective-permute-start | bytes 1179656 | tf_op jit(solution)/shard_map/ppermute | solution.py:38
  (8 other events, 29.4 us)

commit v2 on v0

v2 whole, which is shorter than its diff:
```python
import functools

import jax
import jax.numpy as jnp
from jax import lax
from jax.experimental import pallas as pl
from jax.experimental.pallas import tpu as pltpu
from jax.sharding import PartitionSpec as P

EPS = 1e-05
AXIS = "row"
VMEM_LIMIT = 16 * 1024 * 1024


def plain_per_device(features, activations, norm_gain, gate_weight, up_weight, down_weight):
    float_rows = activations.astype(jnp.float32)
    square_sums = lax.psum(jnp.sum(float_rows * float_rows, axis=1), AXIS)
    inv_scale = lax.rsqrt(square_sums / features + EPS)
    normed = (float_rows * inv_scale[:, None] * norm_gain.astype(jnp.float32)[None, :]).astype(
        jnp.bfloat16
    )
    shard_rows = lax.all_gather(normed, AXIS, axis=1, tiled=True)
    gate_proj = jnp.dot(shard_rows, gate_weight, preferred_element_type=jnp.float32)
    up_proj = jnp.dot(shard_rows, up_weight, preferred_element_type=jnp.float32)
    hidden = (jax.nn.silu(gate_proj) * up_proj).astype(jnp.bfloat16)
    reduced = lax.psum_scatter(
        lax.dot_general(
            down_weight, hidden, (((0,), (1,)), ((), ())), preferred_element_type=jnp.float32
        ),
        AXIS,
        scatter_dimension=0,
        tiled=True,
    )
    return reduced.T.astype(jnp.bfloat16)


def swap(value, mask):
    return lax.ppermute(value, AXIS, [(i, i ^ mask) for i in range(lax.axis_size(AXIS))])


COLS = 256
EXTRA = 16
GATE_UP_SHARE, DOWN_SHARE = (1, 1, 1, 1, 1, 1, 1, 1), 1


def cost(flops, weight_bytes, share):
    return pl.CostEstimate(
        flops=int(flops * share), bytes_accessed=int(weight_bytes * share), transcendentals=0
    )


def fetch(copies):
    for copy in copies:
        copy.start()


def landed(copies):
    for copy in copies:
        copy.wait()


def chip_of(mask):
    return lax.axis_index(AXIS) // 2 ^ mask // 2


def gate_up_fetch(block, gate_hbm, up_hbm, into, sems, cols=slice(None)):
    depth = into.shape[1]
    rows = pl.ds(pl.multiple_of(block * depth, depth), depth)
    return [
        pltpu.make_async_copy(hbm.at[rows, cols], into.at[n, :, cols], sems.at[n])
        for n, hbm in enumerate((gate_hbm, up_hbm))
    ]


def down_fetch(block, down_hbm, into, sems):
    width = into.shape[1]
    cols = pl.ds(pl.multiple_of(block * width, width), width)
    return [pltpu.make_async_copy(down_hbm.at[:, cols], into, sems.at[0])]


def gate_up_kernel(features, first, last, ahead, mine, other, *refs):
    refs = list(refs)
    if first:
        w_now, now_sems = refs.pop(), refs.pop()
    else:
        w_now, gate_in, up_in, squares_in = (refs.pop(0) for _ in range(4))
    if last:
        down_hbm, hidden_ref, next_w, both, sems = refs
        copies = down_fetch(chip_of(ahead), down_hbm, next_w, sems)
    else:
        gate_hbm, up_hbm, gate_out, up_out, squares_out, *mark, next_w, both, sems = refs
        copies = gate_up_fetch(chip_of(ahead), gate_hbm, up_hbm, next_w, sems)
    if first:

        def fetch_piece(n):
            cols = pl.ds(pl.multiple_of(n * COLS, COLS), COLS)
            return gate_up_fetch(chip_of(0), gate_hbm, up_hbm, w_now, now_sems.at[n], cols)

        for n in range(w_now.shape[2] // COLS):
            fetch(fetch_piece(n))
    fetch(copies)
    width = mine.shape[1]
    tokens = both.shape[0]
    core = lax.axis_index(AXIS) % 2
    squares = 0.0 if first else squares_in[...]
    for which, ref in enumerate((mine, other)):
        start = pl.multiple_of((core ^ which) * width, width)
        both[:, pl.ds(start, width)] = ref[:tokens]
        parts = ref[tokens:].astype(jnp.float32)[: EXTRA // 2]
        squares = squares + jnp.sum(parts[:, :tokens], axis=0, keepdims=True)
    if last:
        inv = lax.rsqrt(squares / features + EPS)
        inv = jnp.transpose(jnp.broadcast_to(inv, (8, tokens)))[:, :1]
    else:
        squares_out[...] = squares
        for ref in mark:
            ref[...] = jnp.zeros_like(ref)
    units = hidden_ref.shape[1] if last else gate_out.shape[1]
    def block(n, _):
        cols = pl.ds(pl.multiple_of(n * COLS, COLS), COLS)
        if first:
            for copy in fetch_piece(n):
                copy.wait()
        gate = jnp.dot(both[...], w_now[0, :, cols], preferred_element_type=jnp.float32)
        up = jnp.dot(both[...], w_now[1, :, cols], preferred_element_type=jnp.float32)
        if not first:
            gate = gate_in[:, cols] + gate
            up = up_in[:, cols] + up
        if last:
            gate = gate * inv
            value = gate / (1.0 + jnp.exp(-gate)) * (up * inv)
            hidden_ref[:, cols] = value.astype(jnp.bfloat16)
        else:
            gate_out[:, cols] = gate
            up_out[:, cols] = up
        return 0

    lax.fori_loop(0, units // COLS, block, 0)
    landed(copies)


def vmem():
    return pl.BlockSpec(memory_space=pltpu.VMEM)


def smem():
    return pl.BlockSpec(memory_space=pltpu.SMEM)


def anywhere():
    return pl.BlockSpec(memory_space=pl.ANY)


def in_hbm():
    return pl.BlockSpec(memory_space=pltpu.HBM)


def in_vmem(value):
    return pltpu.with_memory_space_constraint(value, pltpu.VMEM)


def params():
    return pltpu.CompilerParams(vmem_limit_bytes=VMEM_LIMIT)


def gate_up(ahead, mine, other, w_now, sums, weights, features, marked, last, next_shape, share):
    tokens, width = mine.shape[0] - EXTRA, mine.shape[1]
    units = weights[0].shape[1 - last]
    first = sums is None
    acc = pltpu.VMEM((tokens, units), jnp.float32)
    if last:
        out_shape = [pltpu.VMEM((tokens, units), jnp.bfloat16)]
    else:
        out_shape = [acc, acc, jax.ShapeDtypeStruct((1, tokens), jnp.float32)]
        if marked:
            out_shape.append(jax.ShapeDtypeStruct((EXTRA // 2, width), jnp.bfloat16))
    out_shape.append(pltpu.VMEM(next_shape, jnp.bfloat16))
    scratch = [pltpu.VMEM((tokens, 2 * width), jnp.bfloat16), pltpu.SemaphoreType.DMA((2,))]
    if first:
        scratch.append(pltpu.SemaphoreType.DMA((-(-units // COLS), 2)))
        scratch.append(pltpu.VMEM(next_shape, jnp.bfloat16))
    operands = [mine, other]
    in_specs = [vmem(), vmem()]
    aliases = {}
    if not first:
        operands.append(in_vmem(w_now))
        in_specs.append(vmem())
        if not last:
            aliases = {3: 0, 4: 1, 5: 2}
        operands += [in_vmem(total) for total in sums[:2]] + [sums[2]]
        in_specs += [vmem(), vmem(), vmem()]
    operands += list(weights)
    in_specs += [in_hbm() for _ in weights]
    return pl.pallas_call(
        functools.partial(gate_up_kernel, features, first, last, ahead),
        in_specs=in_specs,
        out_specs=[vmem() for _ in out_shape],
        out_shape=out_shape,
        scratch_shapes=scratch,
        input_output_aliases=aliases,
        compiler_params=params(),
        cost_estimate=cost(8 * tokens * width * units, 8 * width * units, share),
        name="gate_up",
    )(*operands)


def down_kernel(last, deps, ahead, hidden_ref, w_now, *refs):
    refs = list(refs[deps:])
    if not last:
        down_hbm, send_ref, keep_ref, next_w, sems = refs
        copies = down_fetch(chip_of(ahead), down_hbm, next_w, sems)
        fetch(copies)
    else:
        send_ref, keep_ref = refs
    width = send_ref.shape[1]
    core = lax.axis_index(AXIS) % 2
    def block(n, _):
        for which, out in ((1, send_ref), (0, keep_ref)):
            start = pl.multiple_of((core ^ which) * width + n * COLS, COLS)
            product = jnp.dot(
                hidden_ref[...], w_now[:, pl.ds(start, COLS)], preferred_element_type=jnp.float32
            )
            out[:, pl.ds(pl.multiple_of(n * COLS, COLS), COLS)] = product.astype(out.dtype)
        return 0

    lax.fori_loop(0, width // COLS, block, 0)
    if not last:
        landed(copies)


def down(ahead, hidden, w_now, down_weight, width, after):
    tokens, units = hidden.shape
    last = down_weight is None
    out_shape = [
        jax.ShapeDtypeStruct((tokens, width), jnp.bfloat16),
        jax.ShapeDtypeStruct((tokens, width), jnp.float32),
    ]
    operands = [in_vmem(hidden), in_vmem(w_now), *after]
    in_specs = [vmem(), vmem()] + [anywhere() for _ in after]
    scratch = []
    if not last:
        operands.append(down_weight)
        in_specs.append(in_hbm())
        out_shape.append(pltpu.VMEM(w_now.shape, jnp.bfloat16))
        scratch = [pltpu.SemaphoreType.DMA((1,))]
    return pl.pallas_call(
        functools.partial(down_kernel, last, len(after), ahead),
        in_specs=in_specs,
        out_specs=[vmem() for _ in out_shape],
        out_shape=out_shape,
        scratch_shapes=scratch,
        compiler_params=params(),
        cost_estimate=cost(4 * tokens * units * width, 4 * units * width, DOWN_SHARE),
        name="down",
    )(*operands)


def held(chunk, after):
    return lax.dynamic_update_slice(chunk, after, (chunk.shape[0] - after.shape[0], 0))


CORE, X, Z1, Z2, Z3 = 1, 2, 4, 8, 12


def per_device(activations, norm_gain, gate_weight, up_weight, down_weight):
    tokens, width = activations.shape
    features, units = gate_weight.shape

    order = [0, X, Z1, Z1 | X, Z3, Z3 | X, Z2, Z2 | X]
    there, here = X, 0
    blocks = [
        Z2 | there, Z1 | there, Z3 | there, Z2 | here, 0 | there, Z3 | here, Z1 | here, 0 | here
    ]

    gate_weight, up_weight, down_weight = (
        pltpu.with_memory_space_constraint(w, pltpu.HBM)
        for w in (gate_weight, up_weight, down_weight)
    )
    w_now = None
    rows = activations.astype(jnp.float32)
    scaled = (rows * norm_gain.astype(jnp.float32)[None, :]).astype(jnp.bfloat16)
    left = jnp.pad(jnp.sum(rows * rows, axis=1), (0, width - tokens))
    parts = []
    for _ in range(3):
        parts.append(lax.reduce_precision(left, 8, 7))
        left = left - parts[-1]
    extra = jnp.pad(jnp.stack(parts), ((0, EXTRA - 3), (0, 0))).astype(jnp.bfloat16)
    own = jnp.concatenate([scaled, extra])

    raw = {0: own, X: swap(own, X), Z3: swap(own, Z3), Z1: swap(own, Z1)}
    sums = None
    for n, mask in enumerate(order):
        last = n == len(order) - 1
        *sums, w_now = gate_up(
            blocks[0] if last else order[n + 1],
            raw[mask],
            swap(raw[mask], CORE),
            w_now,
            sums,
            (down_weight,) if last else (gate_weight, up_weight),
            features,
            n < 2,
            last,
            (units, 2 * width) if last else (2, 2 * width, units),
            GATE_UP_SHARE[n],
        )
        if n < 2:
            mark = sums.pop()
        if n == 0:
            raw[Z1] = held(raw[Z1], mark)
            raw[Z1 | X] = swap(raw[Z1], X)
        if n == 1:
            raw[Z3] = held(raw[Z3], mark)
            raw[Z2] = swap(raw[Z3], Z1)
            raw[Z3 | X] = swap(raw[Z3], X)
            raw[Z2 | X] = swap(raw[Z2], X)
    hidden = sums[0]

    def down_block(n, after):
        last = n == len(blocks) - 1
        send, keep, *w_next = down(
            0 if last else blocks[n + 1], hidden, w_now, None if last else down_weight,
            width, after,
        )
        return w_next[0] if w_next else None, keep + wide(swap(send, CORE))

    w_now, pair = down_block(0, [])
    over_far = narrow(pair)
    w_now, pair = down_block(1, [])
    turn = narrow(pair)
    w_now, pair = down_block(2, [over_far])
    over_next = narrow(pair)
    w_now, far = down_block(3, [turn])
    far = far + wide(swap(over_far, X))
    w_now, pair = down_block(4, [over_next])
    over_here = narrow(pair + wide(swap(turn, Z1)))
    far = narrow(far)
    w_now, next_far = down_block(5, [far])
    next_far = next_far + wide(swap(over_next, X))
    w_now, near = down_block(6, [over_here])
    next_far = narrow(next_far + wide(swap(far, Z1)))
    _, total = down_block(7, [next_far])
    total = total + wide(swap(narrow(near), Z1)) + wide(swap(over_here, X))
    return narrow(total + wide(swap(next_far, Z3)))


def wide(value):
    return value.astype(jnp.float32)


def narrow(value):
    return value.astype(jnp.bfloat16)


def fits(activations):
    tokens, width = activations.shape
    return tokens % 16 == 0 and tokens <= width


def solution(mesh):
    in_specs = (P("groups", AXIS), P(AXIS), P(None, AXIS), P(None, AXIS), P(AXIS, None))
    out_specs = P("groups", AXIS)

    def body(activations, norm_gain, gate_weight, up_weight, down_weight):
        if mesh.shape[AXIS] == 16 and activations.shape[1] % 128 == 0 and fits(activations):
            run = per_device
        else:
            run = functools.partial(plain_per_device, gate_weight.shape[0])
        return run(activations, norm_gain, gate_weight, up_weight, down_weight)

    return jax.shard_map(
        body, mesh=mesh, in_specs=in_specs, out_specs=out_specs, check_vma=False
    )
```

time: 307 us -> 123 us (0.40)
  waiting for transfers between devices: 196 us -> 32.8 us
  matrix products: 56.1 us -> 0 us
  Pallas kernels: 0 us -> 51.5 us
  blocking collectives: 34.9 us -> 0 us
  starting transfers between devices: 0.04 us -> 33.6 us
  between operations: 13.4 us -> 0.31 us
    reduce_scatter x1 -> x0, waiting for transfers between devices: 133 us -> none  [per_device(): lax.psum_scatter(lax.dot_general(down_weight, hidden, (((0,), (1,)), ((),...]
    all_gather x1 -> x0, waiting for transfers between devices: 63.1 us -> none  [per_device(): shard_rows = lax.all_gather(normed, 'row', axis=1, tiled=True)]
    dot_general x3 -> x0, matrix products: 56.1 us -> none  [the longest x1 19.8 us: per_device(): lax.dot_general(down_weight, hidden, (((0,), (1,)), ((), ())), preferred_...]
    pallas_call x0 -> x16, Pallas kernels: none -> 51.5 us  [the longest x8 35.4 us: gate_up(): pl.pallas_call(functools.partial(gate_up_kernel, features, first, last, a...]
    psum x1 -> x0, blocking collectives: 34.9 us -> none  [per_device(): square_sums = lax.psum(jnp.sum(float_rows * float_rows, axis=1), 'row')]
    ppermute x0 -> x30, starting transfers between devices: none -> 33.6 us  [swap(): lax.ppermute(value, AXIS, [(i, i ^ mask) for i in range(lax.axis_size(AXI...]
    ppermute x0 -> x30, waiting for transfers between devices: none -> 32.8 us  [swap(): lax.ppermute(value, AXIS, [(i, i ^ mask) for i in range(lax.axis_size(AXI...]
  transfers between devices with their start and end apart: 2 -> 30, of which waited for: 2 -> 9; matrix products, arithmetic and copies ran while one was open for 0% -> 1% of each run, Pallas kernels for 0% -> 37%
where the time goes in v2:
time: 123 us; the launch traced here: 122 us
  Pallas kernels  51.5 us (42%)
  starting transfers between devices  33.6 us (27%)
  waiting for transfers between devices  32.8 us (27%)
  other arithmetic  3.94 us (3%)
    pallas_call x8, Pallas kernels, gate_up(): pl.pallas_call(functools.partial(gate_up_kernel, features, first, last, a...  35.4 us
    ppermute x30, starting transfers between devices, swap(): lax.ppermute(value, AXIS, [(i, i ^ mask) for i in range(lax.axis_size(AXI...  33.6 us
    ppermute x30, waiting for transfers between devices, swap(): lax.ppermute(value, AXIS, [(i, i ^ mask) for i in range(lax.axis_size(AXI...  32.8 us
    pallas_call x8, Pallas kernels, down(): pl.pallas_call(functools.partial(down_kernel, last, len(after), ahead), i...  16.1 us
  transfers between devices with their start and end apart: 30, of which 9 were waited for; matrix products, arithmetic and copies ran while one was open for 1% of the time, Pallas kernels for 37%

profile of v2, /device:TPU:0, one launch (start us, length us, event | category | flops | bytes accessed | tf_op | source)
XLA Modules:
  0.0 122.2 jit_solution(6342025775917222051)
XLA Ops:
  2.0 3.0 %collective-permute-start.1 = (bf16[400,512]{1,0:T(8,128)(2,1)S(1)}, bf16[400,512]{1,0:T(8,128)(2,1)S(1)}, u32[]{:S(2)}, u32[]{:S(2)}) collective-permute-start(bf16[400,512]{1,0:T(8,128)(2,1)S(1)} %pad_maximum_fusion.mine), channel_id=1, source_target_pairs={{0,2},{1,3},{2,0},{3,1},{4,6},{5,7},{6,4},{7,5},{8,10},{9,11},{10,... | collective-permute-start | bytes 1228808 | tf_op jit(solution)/shard_map/ppermute | solution.py:38
  6.6 7.9 %collective-permute-done.1.mine = bf16[400,512]{1,0:T(8,128)(2,1)S(1)} collective-permute-done((bf16[400,512]{1,0:T(8,128)(2,1)S(1)}, bf16[400,512]{1,0:T(8,128)(2,1)S(1)}, u32[]{:S(2)}, u32[]{:S(2)}) %collective-permute-start.1) | collective-permute-done | bytes 409632 | tf_op jit(solution)/shard_map/ppermute | solution.py:38
  14.4 3.9 %collective-permute-start = (bf16[400,512]{1,0:T(8,128)(2,1)S(1)}, bf16[400,512]{1,0:T(8,128)(2,1)S(1)}, u32[]{:S(2)}, u32[]{:S(2)}) collective-permute-start(bf16[400,512]{1,0:T(8,128)(2,1)S(1)} %pad_maximum_fusion.mine), channel_id=1, source_target_pairs={{0,12},{1,13},{2,14},{3,15},{4,8},{5,9},{6,10},{7,11},{8,4},{9,5},... | collective-permute-start | bytes 1228808 | tf_op jit(solution)/shard_map/ppermute | solution.py:38
  18.3 5.6 %gate_up.8 = (f32[384,1792]{1,0:T(8,128)S(1)}, f32[384,1792]{1,0:T(8,128)S(1)}, f32[1,384]{1,0:T(1,128)S(1)}, bf16[8,512]{1,0:T(8,128)(2,1)S(1)}, bf16[2,1024,1792]{2,1,0:T(8,128)(2,1)S(1)}) custom-call(bf16[400,512]{1,0:T(8,128)(2,1)S(1)} %pad_maximum_fusion.mine, bf16[400,512]{1,0:T(8,128)(2,1)S(1)} %collective-permute-done.3.other, ...), custom_call_target="tpu_custom_call" | custom-call | flops 2818572288 | bytes 7340032 | tf_op jit(solution)/shard_map/gate_up/pallas_call | solution.py:194
  25.5 4.2 %gate_up.9 = (f32[384,1792]{1,0:T(8,128)S(1)}, f32[384,1792]{1,0:T(8,128)S(1)}, f32[1,384]{1,0:T(1,128)S(1)}, bf16[8,512]{1,0:T(8,128)(2,1)S(1)}, bf16[2,1024,1792]{2,1,0:T(8,128)(2,1)S(1)}) custom-call(bf16[400,512]{1,0:T(8,128)(2,1)S(1)} %collective-permute-done.1.mine, ...), custom_call_target="tpu_custom_call", output_to_operand_aliasing={{0}: (3, {}), {1}: (4, {}), {2}: (5, {})} | custom-call | flops 2818572288 | bytes 7340032 | tf_op jit(solution)/shard_map/gate_up/pallas_call | solution.py:194
  29.7 7.3 %collective-permute-start.4 = (bf16[400,512]{1,0:T(8,128)(2,1)S(1)}, bf16[400,512]{1,0:T(8,128)(2,1)S(1)}, u32[]{:S(2)}, u32[]{:S(2)}) collective-permute-start(bf16[400,512]{1,0:T(8,128)(2,1)S(1)} %constant_dynamic-update-slice_fusion.1.mine), channel_id=1, source_target_pairs={{0,4},{1,5},{2,6},{3,7},{4,0},{5,1},{6,2},{7,3},{8,12},{9,13},{10,... | collective-permute-start | bytes 1228808 | tf_op jit(solution)/shard_map/ppermute | solution.py:38
  38.9 4.2 %gate_up.10 = (f32[384,1792]{1,0:T(8,128)S(1)}, f32[384,1792]{1,0:T(8,128)S(1)}, f32[1,384]{1,0:T(1,128)S(1)}, bf16[2,1024,1792]{2,1,0:T(8,128)(2,1)S(1)}) custom-call(bf16[400,512]{1,0:T(8,128)(2,1)S(1)} %constant_dynamic-update-slice_fusion.mine, ...), custom_call_target="tpu_custom_call", output_to_operand_aliasing={{0}: (3, {}), {1}: (4, {}), {2}: (5, {})} | custom-call | flops 2818572288 | bytes 7340032 | tf_op jit(solution)/shard_map/gate_up/pallas_call | solution.py:194
  43.1 3.1 %collective-permute-done.4.mine = bf16[400,512]{1,0:T(8,128)(2,1)S(1)} collective-permute-done((bf16[400,512]{1,0:T(8,128)(2,1)S(1)}, bf16[400,512]{1,0:T(8,128)(2,1)S(1)}, u32[]{:S(2)}, u32[]{:S(2)}) %collective-permute-start.4) | collective-permute-done | bytes 409632 | tf_op jit(solution)/shard_map/ppermute | solution.py:38
  48.0 4.2 %gate_up.11 = (f32[384,1792]{1,0:T(8,128)S(1)}, f32[384,1792]{1,0:T(8,128)S(1)}, f32[1,384]{1,0:T(1,128)S(1)}, bf16[2,1024,1792]{2,1,0:T(8,128)(2,1)S(1)}) custom-call(bf16[400,512]{1,0:T(8,128)(2,1)S(1)} %collective-permute-done.12.mine, ...), custom_call_target="tpu_custom_call", output_to_operand_aliasing={{0}: (3, {}), {1}: (4, {}), {2}: (5, {})} | custom-call | flops 2818572288 | bytes 7340032 | tf_op jit(solution)/shard_map/gate_up/pallas_call | solution.py:194
  52.2 4.2 %gate_up.12 = (f32[384,1792]{1,0:T(8,128)S(1)}, f32[384,1792]{1,0:T(8,128)S(1)}, f32[1,384]{1,0:T(1,128)S(1)}, bf16[2,1024,1792]{2,1,0:T(8,128)(2,1)S(1)}) custom-call(bf16[400,512]{1,0:T(8,128)(2,1)S(1)} %constant_dynamic-update-slice_fusion.1.mine, ...), custom_call_target="tpu_custom_call", output_to_operand_aliasing={{0}: (3, {}), {1}: (4, {}), {2}: (5, {})} | custom-call | flops 2818572288 | bytes 7340032 | tf_op jit(solution)/shard_map/gate_up/pallas_call | solution.py:194
  58.2 4.2 %gate_up.13 = (f32[384,1792]{1,0:T(8,128)S(1)}, f32[384,1792]{1,0:T(8,128)S(1)}, f32[1,384]{1,0:T(1,128)S(1)}, bf16[2,1024,1792]{2,1,0:T(8,128)(2,1)S(1)}) custom-call(bf16[400,512]{1,0:T(8,128)(2,1)S(1)} %collective-permute-done.8.mine, ...), custom_call_target="tpu_custom_call", output_to_operand_aliasing={{0}: (3, {}), {1}: (4, {}), {2}: (5, {})} | custom-call | flops 2818572288 | bytes 7340032 | tf_op jit(solution)/shard_map/gate_up/pallas_call | solution.py:194
  62.4 4.2 %gate_up.14 = (f32[384,1792]{1,0:T(8,128)S(1)}, f32[384,1792]{1,0:T(8,128)S(1)}, f32[1,384]{1,0:T(1,128)S(1)}, bf16[2,1024,1792]{2,1,0:T(8,128)(2,1)S(1)}) custom-call(bf16[400,512]{1,0:T(8,128)(2,1)S(1)} %collective-permute-done.4.mine, ...), custom_call_target="tpu_custom_call", output_to_operand_aliasing={{0}: (3, {}), {1}: (4, {}), {2}: (5, {})} | custom-call | flops 2818572288 | bytes 7340032 | tf_op jit(solution)/shard_map/gate_up/pallas_call | solution.py:194
  66.5 4.7 %gate_up.15 = (bf16[384,1792]{1,0:T(8,128)(2,1)S(1)}, bf16[1792,1024]{1,0:T(8,128)(2,1)S(1)}) custom-call(bf16[400,512]{1,0:T(8,128)(2,1)S(1)} %collective-permute-done.5.mine, bf16[400,512]{1,0:T(8,128)(2,1)S(1)} %collective-permute-done.6.other, bf16[2,1024,1792]{2,1,0:T(8,128)(2,1)S(1)} %get-tuple-element.86.refs_0_, ...), custom_call_target="tpu_custom_call" | custom-call | flops 2818572288 | bytes 7340032 | tf_op jit(solution)/shard_map/gate_up/pallas_call | solution.py:194
  71.3 2.1 %down.8 = (bf16[384,512]{1,0:T(8,128)(2,1)S(1)}, f32[384,512]{1,0:T(8,128)S(1)}, bf16[1792,1024]{1,0:T(8,128)(2,1)S(1)}) custom-call(bf16[384,1792]{1,0:T(8,128)(2,1)S(1)} %get-tuple-element.90.hidden_ref, bf16[1792,1024]{1,0:T(8,128)(2,1)S(1)} %get-tuple-element.91.w_now, bf16[1792,8192]{1,0:T(8,128)(2,1)} %refs_1_.11), custom_call_target="tpu_custom_call" | custom-call | flops 1409286144 | bytes 3670016 | tf_op jit(solution)/shard_map/down/pallas_call | solution.py:246
  74.0 2.0 %down.9 = (bf16[384,512]{1,0:T(8,128)(2,1)S(1)}, f32[384,512]{1,0:T(8,128)S(1)}, bf16[1792,1024]{1,0:T(8,128)(2,1)S(1)}) custom-call(bf16[384,1792]{1,0:T(8,128)(2,1)S(1)} %get-tuple-element.90.hidden_ref, bf16[1792,1024]{1,0:T(8,128)(2,1)S(1)} %get-tuple-element.92.w_now, bf16[1792,8192]{1,0:T(8,128)(2,1)} %refs_1_.11), custom_call_target="tpu_custom_call" | custom-call | flops 1409286144 | bytes 3670016 | tf_op jit(solution)/shard_map/down/pallas_call | solution.py:246
  77.8 2.0 %down.10 = (bf16[384,512]{1,0:T(8,128)(2,1)S(1)}, f32[384,512]{1,0:T(8,128)S(1)}, bf16[1792,1024]{1,0:T(8,128)(2,1)S(1)}) custom-call(bf16[384,1792]{1,0:T(8,128)(2,1)S(1)} %get-tuple-element.90.hidden_ref, bf16[1792,1024]{1,0:T(8,128)(2,1)S(1)} %get-tuple-element.93.w_now, bf16[384,512]{1,0:T(8,128)(2,1)S(1)} %add_convert_fusion.7.refs_0_, ...), custom_call_target="tpu_custom_call" | custom-call | flops 1409286144 | bytes 3670016 | tf_op jit(solution)/shard_map/down/pallas_call | solution.py:246
  82.0 2.0 %down.11 = (bf16[384,512]{1,0:T(8,128)(2,1)S(1)}, f32[384,512]{1,0:T(8,128)S(1)}, bf16[1792,1024]{1,0:T(8,128)(2,1)S(1)}) custom-call(bf16[384,1792]{1,0:T(8,128)(2,1)S(1)} %get-tuple-element.90.hidden_ref, bf16[1792,1024]{1,0:T(8,128)(2,1)S(1)} %get-tuple-element.96.w_now, bf16[384,512]{1,0:T(8,128)(2,1)S(1)} %add_convert_fusion.6.refs_0_, ...), custom_call_target="tpu_custom_call" | custom-call | flops 1409286144 | bytes 3670016 | tf_op jit(solution)/shard_map/down/pallas_call | solution.py:246
  84.9 2.0 %down.12 = (bf16[384,512]{1,0:T(8,128)(2,1)S(1)}, f32[384,512]{1,0:T(8,128)S(1)}, bf16[1792,1024]{1,0:T(8,128)(2,1)S(1)}) custom-call(bf16[384,1792]{1,0:T(8,128)(2,1)S(1)} %get-tuple-element.90.hidden_ref, bf16[1792,1024]{1,0:T(8,128)(2,1)S(1)} %get-tuple-element.99.w_now, bf16[384,512]{1,0:T(8,128)(2,1)S(1)} %add_convert_fusion.5.refs_0_, ...), custom_call_target="tpu_custom_call" | custom-call | flops 1409286144 | bytes 3670016 | tf_op jit(solution)/shard_map/down/pallas_call | solution.py:246
  90.2 2.0 %down.13 = (bf16[384,512]{1,0:T(8,128)(2,1)S(1)}, f32[384,512]{1,0:T(8,128)S(1)}, bf16[1792,1024]{1,0:T(8,128)(2,1)S(1)}) custom-call(bf16[384,1792]{1,0:T(8,128)(2,1)S(1)} %get-tuple-element.90.hidden_ref, bf16[1792,1024]{1,0:T(8,128)(2,1)S(1)} %get-tuple-element.102.w_now, bf16[384,512]{1,0:T(8,128)(2,1)S(1)} %add_convert_fusion.4.refs_0_, ...), custom_call_target="tpu_custom_call" | custom-call | flops 1409286144 | bytes 3670016 | tf_op jit(solution)/shard_map/down/pallas_call | solution.py:246
  94.0 2.0 %down.14 = (bf16[384,512]{1,0:T(8,128)(2,1)S(1)}, f32[384,512]{1,0:T(8,128)S(1)}, bf16[1792,1024]{1,0:T(8,128)(2,1)S(1)}) custom-call(bf16[384,1792]{1,0:T(8,128)(2,1)S(1)} %get-tuple-element.90.hidden_ref, bf16[1792,1024]{1,0:T(8,128)(2,1)S(1)} %get-tuple-element.105.w_now, bf16[384,512]{1,0:T(8,128)(2,1)S(1)} %add_convert_fusion.3.refs_0_, ...), custom_call_target="tpu_custom_call" | custom-call | flops 1409286144 | bytes 3670016 | tf_op jit(solution)/shard_map/down/pallas_call | solution.py:246
  96.5 3.5 %collective-permute-done.24 = bf16[384,512]{1,0:T(8,128)(2,1)S(1)} collective-permute-done((bf16[384,512]{1,0:T(8,128)(2,1)S(1)}, bf16[384,512]{1,0:T(8,128)(2,1)S(1)}, u32[]{:S(2)}, u32[]{:S(2)}) %collective-permute-start.24) | collective-permute-done | bytes 393248 | tf_op jit(solution)/shard_map/ppermute | solution.py:38
  100.3 2.5 %collective-permute-start.29 = (bf16[384,512]{1,0:T(8,128)(2,1)S(1)}, bf16[384,512]{1,0:T(8,128)(2,1)S(1)}, u32[]{:S(2)}, u32[]{:S(2)}) collective-permute-start(bf16[384,512]{1,0:T(8,128)(2,1)S(1)} %add_convert_fusion.2.refs_0_), channel_id=1, source_target_pairs={{0,12},{1,13},{2,14},{3,15},{4,8},{5,9},{6,10},{7,11},{8,4},{9,5},... | collective-permute-start | bytes 1179656 | tf_op jit(solution)/shard_map/ppermute | solution.py:38
  106.4 7.8 %collective-permute-done.29 = bf16[384,512]{1,0:T(8,128)(2,1)S(1)} collective-permute-done((bf16[384,512]{1,0:T(8,128)(2,1)S(1)}, bf16[384,512]{1,0:T(8,128)(2,1)S(1)}, u32[]{:S(2)}, u32[]{:S(2)}) %collective-permute-start.29) | collective-permute-done | bytes 393248 | tf_op jit(solution)/shard_map/ppermute | solution.py:38
  114.2 7.0 %collective-permute-done.27 = bf16[384,512]{1,0:T(8,128)(2,1)S(1)} collective-permute-done((bf16[384,512]{1,0:T(8,128)(2,1)S(1)}, bf16[384,512]{1,0:T(8,128)(2,1)S(1)}, u32[]{:S(2)}, u32[]{:S(2)}) %collective-permute-start.27) | collective-permute-done | bytes 393248 | tf_op jit(solution)/shard_map/ppermute | solution.py:38
  (70 shorter events, 26.2 us)
Async XLA Ops:
  2.0 12.5 %collective-permute-start.1 = (bf16[400,512]{1,0:T(8,128)(2,1)S(1)}, bf16[400,512]{1,0:T(8,128)(2,1)S(1)}, u32[]{:S(2)}, u32[]{:S(2)}) collective-permute-start(bf16[400,512]{1,0:T(8,128)(2,1)S(1)} %pad_maximum_fusion.mine), channel_id=1, source_target_pairs={{0,2},{1,3},{2,0},{3,1},{4,6},{5,7},{6,4},{7,5},{8,10},{9,11},{10,... | collective-permute-start | bytes 1228808 | tf_op jit(solution)/shard_map/ppermute | solution.py:38
  5.0 13.3 %collective-permute-start.3 = (bf16[400,512]{1,0:T(8,128)(2,1)S(1)}, bf16[400,512]{1,0:T(8,128)(2,1)S(1)}, u32[]{:S(2)}, u32[]{:S(2)}) collective-permute-start(bf16[400,512]{1,0:T(8,128)(2,1)S(1)} %pad_maximum_fusion.mine), channel_id=1, source_target_pairs={{0,1},{1,0},{2,3},{3,2},{4,5},{5,4},{6,7},{7,6},{8,9},{9,8},{10,11... | collective-permute-start | bytes 1228808 | tf_op jit(solution)/shard_map/ppermute | solution.py:38
  5.0 18.9 %collective-permute-start.11 = (bf16[400,512]{1,0:T(8,128)(2,1)S(1)}, bf16[400,512]{1,0:T(8,128)(2,1)S(1)}, u32[]{:S(2)}, u32[]{:S(2)}) collective-permute-start(bf16[400,512]{1,0:T(8,128)(2,1)S(1)} %pad_maximum_fusion.mine), channel_id=1, source_target_pairs={{0,4},{1,5},{2,6},{3,7},{4,0},{5,1},{6,2},{7,3},{8,12},{9,13},{10,... | collective-permute-start | bytes 1228808 | tf_op jit(solution)/shard_map/ppermute | solution.py:38
  14.4 11.0 %collective-permute-start.2 = (bf16[400,512]{1,0:T(8,128)(2,1)S(1)}, bf16[400,512]{1,0:T(8,128)(2,1)S(1)}, u32[]{:S(2)}, u32[]{:S(2)}) collective-permute-start(bf16[400,512]{1,0:T(8,128)(2,1)S(1)} %collective-permute-done.1.mine), channel_id=1, source_target_pairs={{0,1},{1,0},{2,3},{3,2},{4,5},{5,4},{6,7},{7,6},{8,9},{9,8},{10,11... | collective-permute-start | bytes 1228808 | tf_op jit(solution)/shard_map/ppermute | solution.py:38
  14.4 15.2 %collective-permute-start = (bf16[400,512]{1,0:T(8,128)(2,1)S(1)}, bf16[400,512]{1,0:T(8,128)(2,1)S(1)}, u32[]{:S(2)}, u32[]{:S(2)}) collective-permute-start(bf16[400,512]{1,0:T(8,128)(2,1)S(1)} %pad_maximum_fusion.mine), channel_id=1, source_target_pairs={{0,12},{1,13},{2,14},{3,15},{4,8},{5,9},{6,10},{7,11},{8,4},{9,5},... | collective-permute-start | bytes 1228808 | tf_op jit(solution)/shard_map/ppermute | solution.py:38
  23.9 14.5 %collective-permute-start.12 = (bf16[400,512]{1,0:T(8,128)(2,1)S(1)}, bf16[400,512]{1,0:T(8,128)(2,1)S(1)}, u32[]{:S(2)}, u32[]{:S(2)}) collective-permute-start(bf16[400,512]{1,0:T(8,128)(2,1)S(1)} %constant_dynamic-update-slice_fusion.mine), channel_id=1, source_target_pairs={{0,2},{1,3},{2,0},{3,1},{4,6},{5,7},{6,4},{7,5},{8,10},{9,11},{10,... | collective-permute-start | bytes 1228808 | tf_op jit(solution)/shard_map/ppermute | solution.py:38
  25.5 13.5 %collective-permute-start.14 = (bf16[400,512]{1,0:T(8,128)(2,1)S(1)}, bf16[400,512]{1,0:T(8,128)(2,1)S(1)}, u32[]{:S(2)}, u32[]{:S(2)}) collective-permute-start(bf16[400,512]{1,0:T(8,128)(2,1)S(1)} %constant_dynamic-update-slice_fusion.mine), channel_id=1, source_target_pairs={{0,1},{1,0},{2,3},{3,2},{4,5},{5,4},{6,7},{7,6},{8,9},{9,8},{10,11... | collective-permute-start | bytes 1228808 | tf_op jit(solution)/shard_map/ppermute | solution.py:38
  29.7 16.6 %collective-permute-start.4 = (bf16[400,512]{1,0:T(8,128)(2,1)S(1)}, bf16[400,512]{1,0:T(8,128)(2,1)S(1)}, u32[]{:S(2)}, u32[]{:S(2)}) collective-permute-start(bf16[400,512]{1,0:T(8,128)(2,1)S(1)} %constant_dynamic-update-slice_fusion.1.mine), channel_id=1, source_target_pairs={{0,4},{1,5},{2,6},{3,7},{4,0},{5,1},{6,2},{7,3},{8,12},{9,13},{10,... | collective-permute-start | bytes 1228808 | tf_op jit(solution)/shard_map/ppermute | solution.py:38
  36.9 10.9 %collective-permute-start.8 = (bf16[400,512]{1,0:T(8,128)(2,1)S(1)}, bf16[400,512]{1,0:T(8,128)(2,1)S(1)}, u32[]{:S(2)}, u32[]{:S(2)}) collective-permute-start(bf16[400,512]{1,0:T(8,128)(2,1)S(1)} %constant_dynamic-update-slice_fusion.1.mine), channel_id=1, source_target_pairs={{0,2},{1,3},{2,0},{3,1},{4,6},{5,7},{6,4},{7,5},{8,10},{9,11},{10,... | collective-permute-start | bytes 1228808 | tf_op jit(solution)/shard_map/ppermute | solution.py:38
  38.4 9.6 %collective-permute-start.13 = (bf16[400,512]{1,0:T(8,128)(2,1)S(1)}, bf16[400,512]{1,0:T(8,128)(2,1)S(1)}, u32[]{:S(2)}, u32[]{:S(2)}) collective-permute-start(bf16[400,512]{1,0:T(8,128)(2,1)S(1)} %collective-permute-done.12.mine), channel_id=1, source_target_pairs={{0,1},{1,0},{2,3},{3,2},{4,5},{5,4},{6,7},{7,6},{8,9},{9,8},{10,11... | collective-permute-start | bytes 1228808 | tf_op jit(solution)/shard_map/ppermute | solution.py:38
  38.4 13.8 %collective-permute-start.10 = (bf16[400,512]{1,0:T(8,128)(2,1)S(1)}, bf16[400,512]{1,0:T(8,128)(2,1)S(1)}, u32[]{:S(2)}, u32[]{:S(2)}) collective-permute-start(bf16[400,512]{1,0:T(8,128)(2,1)S(1)} %constant_dynamic-update-slice_fusion.1.mine), channel_id=1, source_target_pairs={{0,1},{1,0},{2,3},{3,2},{4,5},{5,4},{6,7},{7,6},{8,9},{9,8},{10,11... | collective-permute-start | bytes 1228808 | tf_op jit(solution)/shard_map/ppermute | solution.py:38
  46.3 16.1 %collective-permute-start.7 = (bf16[400,512]{1,0:T(8,128)(2,1)S(1)}, bf16[400,512]{1,0:T(8,128)(2,1)S(1)}, u32[]{:S(2)}, u32[]{:S(2)}) collective-permute-start(bf16[400,512]{1,0:T(8,128)(2,1)S(1)} %collective-permute-done.4.mine), channel_id=1, source_target_pairs={{0,1},{1,0},{2,3},{3,2},{4,5},{5,4},{6,7},{7,6},{8,9},{9,8},{10,11... | collective-permute-start | bytes 1228808 | tf_op jit(solution)/shard_map/ppermute | solution.py:38
  46.3 11.9 %collective-permute-start.5 = (bf16[400,512]{1,0:T(8,128)(2,1)S(1)}, bf16[400,512]{1,0:T(8,128)(2,1)S(1)}, u32[]{:S(2)}, u32[]{:S(2)}) collective-permute-start(bf16[400,512]{1,0:T(8,128)(2,1)S(1)} %collective-permute-done.4.mine), channel_id=1, source_target_pairs={{0,2},{1,3},{2,0},{3,1},{4,6},{5,7},{6,4},{7,5},{8,10},{9,11},{10,... | collective-permute-start | bytes 1228808 | tf_op jit(solution)/shard_map/ppermute | solution.py:38
  47.8 10.4 %collective-permute-start.9 = (bf16[400,512]{1,0:T(8,128)(2,1)S(1)}, bf16[400,512]{1,0:T(8,128)(2,1)S(1)}, u32[]{:S(2)}, u32[]{:S(2)}) collective-permute-start(bf16[400,512]{1,0:T(8,128)(2,1)S(1)} %collective-permute-done.8.mine), channel_id=1, source_target_pairs={{0,1},{1,0},{2,3},{3,2},{4,5},{5,4},{6,7},{7,6},{8,9},{9,8},{10,11... | collective-permute-start | bytes 1228808 | tf_op jit(solution)/shard_map/ppermute | solution.py:38
  58.2 8.4 %collective-permute-start.6 = (bf16[400,512]{1,0:T(8,128)(2,1)S(1)}, bf16[400,512]{1,0:T(8,128)(2,1)S(1)}, u32[]{:S(2)}, u32[]{:S(2)}) collective-permute-start(bf16[400,512]{1,0:T(8,128)(2,1)S(1)} %collective-permute-done.5.mine), channel_id=1, source_target_pairs={{0,1},{1,0},{2,3},{3,2},{4,5},{5,4},{6,7},{7,6},{8,9},{9,8},{10,11... | collective-permute-start | bytes 1228808 | tf_op jit(solution)/shard_map/ppermute | solution.py:38
  76.2 11.9 %collective-permute-start.19 = (bf16[384,512]{1,0:T(8,128)(2,1)S(1)}, bf16[384,512]{1,0:T(8,128)(2,1)S(1)}, u32[]{:S(2)}, u32[]{:S(2)}) collective-permute-start(bf16[384,512]{1,0:T(8,128)(2,1)S(1)} %add_convert_fusion.7.refs_0_), channel_id=1, source_target_pairs={{0,2},{1,3},{2,0},{3,1},{4,6},{5,7},{6,4},{7,5},{8,10},{9,11},{10,... | collective-permute-start | bytes 1179656 | tf_op jit(solution)/shard_map/ppermute | solution.py:38
  80.2 12.1 %collective-permute-start.21 = (bf16[384,512]{1,0:T(8,128)(2,1)S(1)}, bf16[384,512]{1,0:T(8,128)(2,1)S(1)}, u32[]{:S(2)}, u32[]{:S(2)}) collective-permute-start(bf16[384,512]{1,0:T(8,128)(2,1)S(1)} %add_convert_fusion.6.refs_0_), channel_id=1, source_target_pairs={{0,4},{1,5},{2,6},{3,7},{4,0},{5,1},{6,2},{7,3},{8,12},{9,13},{10,... | collective-permute-start | bytes 1179656 | tf_op jit(solution)/shard_map/ppermute | solution.py:38
  84.3 12.2 %collective-permute-start.23 = (bf16[384,512]{1,0:T(8,128)(2,1)S(1)}, bf16[384,512]{1,0:T(8,128)(2,1)S(1)}, u32[]{:S(2)}, u32[]{:S(2)}) collective-permute-start(bf16[384,512]{1,0:T(8,128)(2,1)S(1)} %add_convert_fusion.5.refs_0_), channel_id=1, source_target_pairs={{0,2},{1,3},{2,0},{3,1},{4,6},{5,7},{6,4},{7,5},{8,10},{9,11},{10,... | collective-permute-start | bytes 1179656 | tf_op jit(solution)/shard_map/ppermute | solution.py:38
  87.0 5.4 %collective-permute-start.20 = (bf16[384,512]{1,0:T(8,128)(2,1)S(1)}, bf16[384,512]{1,0:T(8,128)(2,1)S(1)}, u32[]{:S(2)}, u32[]{:S(2)}) collective-permute-start(bf16[384,512]{1,0:T(8,128)(2,1)S(1)} %get-tuple-element.107), channel_id=1, source_target_pairs={{0,1},{1,0},{2,3},{3,2},{4,5},{5,4},{6,7},{7,6},{8,9},{9,8},{10,11... | collective-permute-start | bytes 1179656 | tf_op jit(solution)/shard_map/ppermute | solution.py:38
  88.3 11.8 %collective-permute-start.24 = (bf16[384,512]{1,0:T(8,128)(2,1)S(1)}, bf16[384,512]{1,0:T(8,128)(2,1)S(1)}, u32[]{:S(2)}, u32[]{:S(2)}) collective-permute-start(bf16[384,512]{1,0:T(8,128)(2,1)S(1)} %add_convert_fusion.4.refs_0_), channel_id=1, source_target_pairs={{0,4},{1,5},{2,6},{3,7},{4,0},{5,1},{6,2},{7,3},{8,12},{9,13},{10,... | collective-permute-start | bytes 1179656 | tf_op jit(solution)/shard_map/ppermute | solution.py:38
  92.5 13.9 %collective-permute-start.28 = (bf16[384,512]{1,0:T(8,128)(2,1)S(1)}, bf16[384,512]{1,0:T(8,128)(2,1)S(1)}, u32[]{:S(2)}, u32[]{:S(2)}) collective-permute-start(bf16[384,512]{1,0:T(8,128)(2,1)S(1)} %add_convert_fusion.3.refs_0_), channel_id=1, source_target_pairs={{0,2},{1,3},{2,0},{3,1},{4,6},{5,7},{6,4},{7,5},{8,10},{9,11},{10,... | collective-permute-start | bytes 1179656 | tf_op jit(solution)/shard_map/ppermute | solution.py:38
  96.1 8.6 %collective-permute-start.26 = (bf16[384,512]{1,0:T(8,128)(2,1)S(1)}, bf16[384,512]{1,0:T(8,128)(2,1)S(1)}, u32[]{:S(2)}, u32[]{:S(2)}) collective-permute-start(bf16[384,512]{1,0:T(8,128)(2,1)S(1)} %get-tuple-element.114), channel_id=1, source_target_pairs={{0,1},{1,0},{2,3},{3,2},{4,5},{5,4},{6,7},{7,6},{8,9},{9,8},{10,11... | collective-permute-start | bytes 1179656 | tf_op jit(solution)/shard_map/ppermute | solution.py:38
  100.3 14.0 %collective-permute-start.29 = (bf16[384,512]{1,0:T(8,128)(2,1)S(1)}, bf16[384,512]{1,0:T(8,128)(2,1)S(1)}, u32[]{:S(2)}, u32[]{:S(2)}) collective-permute-start(bf16[384,512]{1,0:T(8,128)(2,1)S(1)} %add_convert_fusion.2.refs_0_), channel_id=1, source_target_pairs={{0,12},{1,13},{2,14},{3,15},{4,8},{5,9},{6,10},{7,11},{8,4},{9,5},... | collective-permute-start | bytes 1179656 | tf_op jit(solution)/shard_map/ppermute | solution.py:38
  104.8 16.3 %collective-permute-start.27 = (bf16[384,512]{1,0:T(8,128)(2,1)S(1)}, bf16[384,512]{1,0:T(8,128)(2,1)S(1)}, u32[]{:S(2)}, u32[]{:S(2)}) collective-permute-start(bf16[384,512]{1,0:T(8,128)(2,1)S(1)} %add_convert_fusion.1), channel_id=1, source_target_pairs={{0,4},{1,5},{2,6},{3,7},{4,0},{5,1},{6,2},{7,3},{8,12},{9,13},{10,... | collective-permute-start | bytes 1179656 | tf_op jit(solution)/shard_map/ppermute | solution.py:38
  (6 other events, 20.3 us)

commit v3 on v2

--- a/solution.py
+++ b/solution.py
@@ -40,7 +40,7 @@
 
 COLS = 256
 EXTRA = 16
-GATE_UP_SHARE, DOWN_SHARE = (1, 1, 1, 1, 1, 1, 1, 1), 1
+FIRST_SHARE, GATE_UP_SHARE, DOWN_SHARE = 4, (2, 2, 2, 2, 2, 2, 2, 2), 3
 
 
 def cost(flops, weight_bytes, share):
@@ -78,26 +78,24 @@
     return [pltpu.make_async_copy(down_hbm.at[:, cols], into, sems.at[0])]
 
 
+def first_fetch_kernel(gate_hbm, up_hbm, mark, next_w, sems):
+    copies = gate_up_fetch(chip_of(0), gate_hbm, up_hbm, next_w, sems)
+    fetch(copies)
+    mark[...] = jnp.zeros_like(mark)
+    landed(copies)
+
+
 def gate_up_kernel(features, first, last, ahead, mine, other, *refs):
     refs = list(refs)
-    if first:
-        w_now, now_sems = refs.pop(), refs.pop()
-    else:
-        w_now, gate_in, up_in, squares_in = (refs.pop(0) for _ in range(4))
+    w_now = refs.pop(0)
+    if not first:
+        gate_in, up_in, squares_in = refs.pop(0), refs.pop(0), refs.pop(0)
     if last:
         down_hbm, hidden_ref, next_w, both, sems = refs
         copies = down_fetch(chip_of(ahead), down_hbm, next_w, sems)
     else:
         gate_hbm, up_hbm, gate_out, up_out, squares_out, *mark, next_w, both, sems = refs
         copies = gate_up_fetch(chip_of(ahead), gate_hbm, up_hbm, next_w, sems)
-    if first:
-
-        def fetch_piece(n):
-            cols = pl.ds(pl.multiple_of(n * COLS, COLS), COLS)
-            return gate_up_fetch(chip_of(0), gate_hbm, up_hbm, w_now, now_sems.at[n], cols)
-
-        for n in range(w_now.shape[2] // COLS):
-            fetch(fetch_piece(n))
     fetch(copies)
     width = mine.shape[1]
     tokens = both.shape[0]
@@ -118,9 +116,6 @@
     units = hidden_ref.shape[1] if last else gate_out.shape[1]
     def block(n, _):
         cols = pl.ds(pl.multiple_of(n * COLS, COLS), COLS)
-        if first:
-            for copy in fetch_piece(n):
-                copy.wait()
         gate = jnp.dot(both[...], w_now[0, :, cols], preferred_element_type=jnp.float32)
         up = jnp.dot(both[...], w_now[1, :, cols], preferred_element_type=jnp.float32)
         if not first:
@@ -163,6 +158,23 @@
     return pltpu.CompilerParams(vmem_limit_bytes=VMEM_LIMIT)
 
 
+def first_fetch(gate_weight, up_weight, width):
+    units = gate_weight.shape[1]
+    return pl.pallas_call(
+        first_fetch_kernel,
+        in_specs=[in_hbm(), in_hbm()],
+        out_specs=[vmem(), vmem()],
+        out_shape=[
+            jax.ShapeDtypeStruct((EXTRA // 2, width), jnp.bfloat16),
+            pltpu.VMEM((2, 2 * width, units), jnp.bfloat16),
+        ],
+        scratch_shapes=[pltpu.SemaphoreType.DMA((2,))],
+        compiler_params=params(),
+        cost_estimate=cost(0, 8 * width * units, FIRST_SHARE),
+        name="first_fetch",
+    )(gate_weight, up_weight)
+
+
 def gate_up(ahead, mine, other, w_now, sums, weights, features, marked, last, next_shape, share):
     tokens, width = mine.shape[0] - EXTRA, mine.shape[1]
     units = weights[0].shape[1 - last]
@@ -176,15 +188,10 @@
             out_shape.append(jax.ShapeDtypeStruct((EXTRA // 2, width), jnp.bfloat16))
     out_shape.append(pltpu.VMEM(next_shape, jnp.bfloat16))
     scratch = [pltpu.VMEM((tokens, 2 * width), jnp.bfloat16), pltpu.SemaphoreType.DMA((2,))]
-    if first:
-        scratch.append(pltpu.SemaphoreType.DMA((-(-units // COLS), 2)))
-        scratch.append(pltpu.VMEM(next_shape, jnp.bfloat16))
-    operands = [mine, other]
-    in_specs = [vmem(), vmem()]
+    operands = [mine, other, in_vmem(w_now)]
+    in_specs = [vmem(), vmem(), vmem()]
     aliases = {}
     if not first:
-        operands.append(in_vmem(w_now))
-        in_specs.append(vmem())
         if not last:
             aliases = {3: 0, 4: 1, 5: 2}
         operands += [in_vmem(total) for total in sums[:2]] + [sums[2]]
@@ -276,7 +283,7 @@
         pltpu.with_memory_space_constraint(w, pltpu.HBM)
         for w in (gate_weight, up_weight, down_weight)
     )
-    w_now = None
+    mark, w_now = first_fetch(gate_weight, up_weight, width)
     rows = activations.astype(jnp.float32)
     scaled = (rows * norm_gain.astype(jnp.float32)[None, :]).astype(jnp.bfloat16)
     left = jnp.pad(jnp.sum(rows * rows, axis=1), (0, width - tokens))
@@ -288,7 +295,7 @@
     own = jnp.concatenate([scaled, extra])
 
     raw = {0: own, X: swap(own, X), Z3: swap(own, Z3), Z1: swap(own, Z1)}
-    sums = None
+    sums, marked = None, (0, 1, 3, 5)
     for n, mask in enumerate(order):
         last = n == len(order) - 1
         *sums, w_now = gate_up(
@@ -299,12 +306,12 @@
             sums,
             (down_weight,) if last else (gate_weight, up_weight),
             features,
-            n < 2,
+            n in marked,
             last,
             (units, 2 * width) if last else (2, 2 * width, units),
             GATE_UP_SHARE[n],
         )
-        if n < 2:
+        if n in marked:
             mark = sums.pop()
         if n == 0:
             raw[Z1] = held(raw[Z1], mark)
@@ -313,7 +320,11 @@
             raw[Z3] = held(raw[Z3], mark)
             raw[Z2] = swap(raw[Z3], Z1)
             raw[Z3 | X] = swap(raw[Z3], X)
+        if n == 3:
+            raw[Z2] = held(raw[Z2], mark)
             raw[Z2 | X] = swap(raw[Z2], X)
+        if n == 5:
+            raw[Z2 | X] = held(raw[Z2 | X], mark)
     hidden = sums[0]
 
     def down_block(n, after):

time: 123 us -> 117 us (0.951)
  waiting for transfers between devices: 32.8 us -> 27.2 us
  starting transfers between devices: 33.6 us -> 31.1 us
  Pallas kernels: 51.5 us -> 53.9 us
    ppermute x30, waiting for transfers between devices: 32.8 us -> 27.2 us  [swap(): lax.ppermute(value, AXIS, [(i, i ^ mask) for i in range(lax.axis_size(AXI...]
    pallas_call x0 -> x1, Pallas kernels: none -> 3.77 us  [first_fetch(): pl.pallas_call(first_fetch_kernel, in_specs=[in_hbm(), in_hbm()], out_spe...]
    ppermute x30, starting transfers between devices: 33.6 us -> 31.1 us  [swap(): lax.ppermute(value, AXIS, [(i, i ^ mask) for i in range(lax.axis_size(AXI...]
    pallas_call x8, Pallas kernels: 35.4 us -> 34 us  [gate_up(): pl.pallas_call(functools.partial(gate_up_kernel, features, first, last, a...]
  transfers between devices with their start and end apart: 30 -> 30, of which waited for: 9 -> 11; matrix products, arithmetic and copies ran while one was open for 1% -> 1% of each run, Pallas kernels for 37% -> 40%
where the time goes in v3:
time: 117 us; the launch traced here: 116 us
  Pallas kernels  53.9 us (46%)
  starting transfers between devices  31.1 us (27%)
  waiting for transfers between devices  27.2 us (23%)
  other arithmetic  3.94 us (3%)
    pallas_call x8, Pallas kernels, gate_up(): pl.pallas_call(functools.partial(gate_up_kernel, features, first, last, a...  34 us
    ppermute x30, starting transfers between devices, swap(): lax.ppermute(value, AXIS, [(i, i ^ mask) for i in range(lax.axis_size(AXI...  31.1 us
    ppermute x30, waiting for transfers between devices, swap(): lax.ppermute(value, AXIS, [(i, i ^ mask) for i in range(lax.axis_size(AXI...  27.2 us
    pallas_call x8, Pallas kernels, down(): pl.pallas_call(functools.partial(down_kernel, last, len(after), ahead), i...  16.1 us
    pallas_call x1, Pallas kernels, first_fetch(): pl.pallas_call(first_fetch_kernel, in_specs=[in_hbm(), in_hbm()], out_spe...  3.77 us
  transfers between devices with their start and end apart: 30, of which 11 were waited for; matrix products, arithmetic and copies ran while one was open for 1% of the time, Pallas kernels for 40%

profile of v3, /device:TPU:0, one launch (start us, length us, event | category | flops | bytes accessed | tf_op | source)
XLA Modules:
  0.0 116.5 jit_solution(12825493681885548666)
XLA Ops:
  2.0 3.0 %collective-permute-start.1 = (bf16[400,512]{1,0:T(8,128)(2,1)S(1)}, bf16[400,512]{1,0:T(8,128)(2,1)S(1)}, u32[]{:S(2)}, u32[]{:S(2)}) collective-permute-start(bf16[400,512]{1,0:T(8,128)(2,1)S(1)} %pad_maximum_fusion.mine), channel_id=1, source_target_pairs={{0,2},{1,3},{2,0},{3,1},{4,6},{5,7},{6,4},{7,5},{8,10},{9,11},{10,... | collective-permute-start | bytes 1228808 | tf_op jit(solution)/shard_map/ppermute | solution.py:38
  6.6 2.5 %collective-permute-start = (bf16[400,512]{1,0:T(8,128)(2,1)S(1)}, bf16[400,512]{1,0:T(8,128)(2,1)S(1)}, u32[]{:S(2)}, u32[]{:S(2)}) collective-permute-start(bf16[400,512]{1,0:T(8,128)(2,1)S(1)} %pad_maximum_fusion.mine), channel_id=1, source_target_pairs={{0,12},{1,13},{2,14},{3,15},{4,8},{5,9},{6,10},{7,11},{8,4},{9,5},... | collective-permute-start | bytes 1228808 | tf_op jit(solution)/shard_map/ppermute | solution.py:38
  9.0 3.8 %first_fetch.1 = (bf16[8,512]{1,0:T(8,128)(2,1)}, bf16[2,1024,1792]{2,1,0:T(8,128)(2,1)S(1)}) custom-call(bf16[8192,1792]{1,0:T(8,128)(2,1)} %refs_4_.12, bf16[8192,1792]{1,0:T(8,128)(2,1)} %refs_5_.11), custom_call_target="tpu_custom_call" | custom-call | bytes 29360128 | tf_op jit(solution)/shard_map/first_fetch/pallas_call | solution.py:163
  14.4 4.2 %gate_up.8 = (f32[384,1792]{1,0:T(8,128)S(1)}, f32[384,1792]{1,0:T(8,128)S(1)}, f32[1,384]{1,0:T(1,128)S(1)}, bf16[8,512]{1,0:T(8,128)(2,1)S(1)}, bf16[2,1024,1792]{2,1,0:T(8,128)(2,1)S(1)}) custom-call(bf16[400,512]{1,0:T(8,128)(2,1)S(1)} %pad_maximum_fusion.mine, bf16[400,512]{1,0:T(8,128)(2,1)S(1)} %collective-permute-done.3.other, ...), custom_call_target="tpu_custom_call" | custom-call | flops 5637144576 | bytes 14680064 | tf_op jit(solution)/shard_map/gate_up/pallas_call | solution.py:201
  21.0 4.2 %gate_up.9 = (f32[384,1792]{1,0:T(8,128)S(1)}, f32[384,1792]{1,0:T(8,128)S(1)}, f32[1,384]{1,0:T(1,128)S(1)}, bf16[8,512]{1,0:T(8,128)(2,1)S(1)}, bf16[2,1024,1792]{2,1,0:T(8,128)(2,1)S(1)}) custom-call(bf16[400,512]{1,0:T(8,128)(2,1)S(1)} %collective-permute-done.1.mine, ...), custom_call_target="tpu_custom_call", output_to_operand_aliasing={{0}: (3, {}), {1}: (4, {}), {2}: (5, {})} | custom-call | flops 5637144576 | bytes 14680064 | tf_op jit(solution)/shard_map/gate_up/pallas_call | solution.py:201
  25.1 2.6 %collective-permute-done = bf16[400,512]{1,0:T(8,128)(2,1)S(1)} collective-permute-done((bf16[400,512]{1,0:T(8,128)(2,1)S(1)}, bf16[400,512]{1,0:T(8,128)(2,1)S(1)}, u32[]{:S(2)}, u32[]{:S(2)}) %collective-permute-start) | collective-permute-done | bytes 409632 | tf_op jit(solution)/shard_map/ppermute | solution.py:38
  30.8 4.2 %gate_up.10 = (f32[384,1792]{1,0:T(8,128)S(1)}, f32[384,1792]{1,0:T(8,128)S(1)}, f32[1,384]{1,0:T(1,128)S(1)}, bf16[2,1024,1792]{2,1,0:T(8,128)(2,1)S(1)}) custom-call(bf16[400,512]{1,0:T(8,128)(2,1)S(1)} %constant_dynamic-update-slice_fusion.2.mine, ...), custom_call_target="tpu_custom_call", output_to_operand_aliasing={{0}: (3, {}), {1}: (4, {}), {2}: (5, {})} | custom-call | flops 5637144576 | bytes 14680064 | tf_op jit(solution)/shard_map/gate_up/pallas_call | solution.py:201
  35.0 4.2 %gate_up.11 = (f32[384,1792]{1,0:T(8,128)S(1)}, f32[384,1792]{1,0:T(8,128)S(1)}, f32[1,384]{1,0:T(1,128)S(1)}, bf16[8,512]{1,0:T(8,128)(2,1)S(1)}, bf16[2,1024,1792]{2,1,0:T(8,128)(2,1)S(1)}) custom-call(bf16[400,512]{1,0:T(8,128)(2,1)S(1)} %collective-permute-done.6.mine, ...), custom_call_target="tpu_custom_call", output_to_operand_aliasing={{0}: (3, {}), {1}: (4, {}), {2}: (5, {})} | custom-call | flops 5637144576 | bytes 14680064 | tf_op jit(solution)/shard_map/gate_up/pallas_call | solution.py:201
  39.9 2.4 %collective-permute-start.9 = (bf16[400,512]{1,0:T(8,128)(2,1)S(1)}, bf16[400,512]{1,0:T(8,128)(2,1)S(1)}, u32[]{:S(2)}, u32[]{:S(2)}) collective-permute-start(bf16[400,512]{1,0:T(8,128)(2,1)S(1)} %constant_dynamic-update-slice_fusion.1.mine), channel_id=1, source_target_pairs={{0,2},{1,3},{2,0},{3,1},{4,6},{5,7},{6,4},{7,5},{8,10},{9,11},{10,... | collective-permute-start | bytes 1228808 | tf_op jit(solution)/shard_map/ppermute | solution.py:38
  42.3 4.2 %gate_up.12 = (f32[384,1792]{1,0:T(8,128)S(1)}, f32[384,1792]{1,0:T(8,128)S(1)}, f32[1,384]{1,0:T(1,128)S(1)}, bf16[2,1024,1792]{2,1,0:T(8,128)(2,1)S(1)}) custom-call(bf16[400,512]{1,0:T(8,128)(2,1)S(1)} %constant_dynamic-update-slice_fusion.3.mine, ...), custom_call_target="tpu_custom_call", output_to_operand_aliasing={{0}: (3, {}), {1}: (4, {}), {2}: (5, {})} | custom-call | flops 5637144576 | bytes 14680064 | tf_op jit(solution)/shard_map/gate_up/pallas_call | solution.py:201
  46.5 4.2 %gate_up.13 = (f32[384,1792]{1,0:T(8,128)S(1)}, f32[384,1792]{1,0:T(8,128)S(1)}, f32[1,384]{1,0:T(1,128)S(1)}, bf16[8,512]{1,0:T(8,128)(2,1)S(1)}, bf16[2,1024,1792]{2,1,0:T(8,128)(2,1)S(1)}) custom-call(bf16[400,512]{1,0:T(8,128)(2,1)S(1)} %collective-permute-done.10.mine, ...), custom_call_target="tpu_custom_call", output_to_operand_aliasing={{0}: (3, {}), {1}: (4, {}), {2}: (5, {})} | custom-call | flops 5637144576 | bytes 14680064 | tf_op jit(solution)/shard_map/gate_up/pallas_call | solution.py:201
  52.0 4.2 %gate_up.14 = (f32[384,1792]{1,0:T(8,128)S(1)}, f32[384,1792]{1,0:T(8,128)S(1)}, f32[1,384]{1,0:T(1,128)S(1)}, bf16[2,1024,1792]{2,1,0:T(8,128)(2,1)S(1)}) custom-call(bf16[400,512]{1,0:T(8,128)(2,1)S(1)} %constant_dynamic-update-slice_fusion.1.mine, ...), custom_call_target="tpu_custom_call", output_to_operand_aliasing={{0}: (3, {}), {1}: (4, {}), {2}: (5, {})} | custom-call | flops 5637144576 | bytes 14680064 | tf_op jit(solution)/shard_map/gate_up/pallas_call | solution.py:201
  56.2 4.7 %gate_up.15 = (bf16[384,1792]{1,0:T(8,128)(2,1)S(1)}, bf16[1792,1024]{1,0:T(8,128)(2,1)S(1)}) custom-call(bf16[400,512]{1,0:T(8,128)(2,1)S(1)} %constant_dynamic-update-slice_fusion.mine, bf16[400,512]{1,0:T(8,128)(2,1)S(1)} %collective-permute-done.13.other, bf16[2,1024,1792]{2,1,0:T(8,128)(2,1)S(1)} %get-tuple-element.92.refs_0_, ...), custom_call_target="tpu_custom_call" | custom-call | flops 5637144576 | bytes 14680064 | tf_op jit(solution)/shard_map/gate_up/pallas_call | solution.py:201
  61.0 2.1 %down.8 = (bf16[384,512]{1,0:T(8,128)(2,1)S(1)}, f32[384,512]{1,0:T(8,128)S(1)}, bf16[1792,1024]{1,0:T(8,128)(2,1)S(1)}) custom-call(bf16[384,1792]{1,0:T(8,128)(2,1)S(1)} %get-tuple-element.96.hidden_ref, bf16[1792,1024]{1,0:T(8,128)(2,1)S(1)} %get-tuple-element.97.w_now, bf16[1792,8192]{1,0:T(8,128)(2,1)} %refs_1_.11), custom_call_target="tpu_custom_call" | custom-call | flops 4227858432 | bytes 11010048 | tf_op jit(solution)/shard_map/down/pallas_call | solution.py:253
  63.6 2.0 %down.9 = (bf16[384,512]{1,0:T(8,128)(2,1)S(1)}, f32[384,512]{1,0:T(8,128)S(1)}, bf16[1792,1024]{1,0:T(8,128)(2,1)S(1)}) custom-call(bf16[384,1792]{1,0:T(8,128)(2,1)S(1)} %get-tuple-element.96.hidden_ref, bf16[1792,1024]{1,0:T(8,128)(2,1)S(1)} %get-tuple-element.98.w_now, bf16[1792,8192]{1,0:T(8,128)(2,1)} %refs_1_.11), custom_call_target="tpu_custom_call" | custom-call | flops 4227858432 | bytes 11010048 | tf_op jit(solution)/shard_map/down/pallas_call | solution.py:253
  67.7 2.0 %down.10 = (bf16[384,512]{1,0:T(8,128)(2,1)S(1)}, f32[384,512]{1,0:T(8,128)S(1)}, bf16[1792,1024]{1,0:T(8,128)(2,1)S(1)}) custom-call(bf16[384,1792]{1,0:T(8,128)(2,1)S(1)} %get-tuple-element.96.hidden_ref, bf16[1792,1024]{1,0:T(8,128)(2,1)S(1)} %get-tuple-element.99.w_now, bf16[384,512]{1,0:T(8,128)(2,1)S(1)} %add_convert_fusion.7.refs_0_, ...), custom_call_target="tpu_custom_call" | custom-call | flops 4227858432 | bytes 11010048 | tf_op jit(solution)/shard_map/down/pallas_call | solution.py:253
  71.8 2.0 %down.11 = (bf16[384,512]{1,0:T(8,128)(2,1)S(1)}, f32[384,512]{1,0:T(8,128)S(1)}, bf16[1792,1024]{1,0:T(8,128)(2,1)S(1)}) custom-call(bf16[384,1792]{1,0:T(8,128)(2,1)S(1)} %get-tuple-element.96.hidden_ref, bf16[1792,1024]{1,0:T(8,128)(2,1)S(1)} %get-tuple-element.102.w_now, bf16[384,512]{1,0:T(8,128)(2,1)S(1)} %add_convert_fusion.6.refs_0_, ...), custom_call_target="tpu_custom_call" | custom-call | flops 4227858432 | bytes 11010048 | tf_op jit(solution)/shard_map/down/pallas_call | solution.py:253
  74.6 2.0 %down.12 = (bf16[384,512]{1,0:T(8,128)(2,1)S(1)}, f32[384,512]{1,0:T(8,128)S(1)}, bf16[1792,1024]{1,0:T(8,128)(2,1)S(1)}) custom-call(bf16[384,1792]{1,0:T(8,128)(2,1)S(1)} %get-tuple-element.96.hidden_ref, bf16[1792,1024]{1,0:T(8,128)(2,1)S(1)} %get-tuple-element.105.w_now, bf16[384,512]{1,0:T(8,128)(2,1)S(1)} %add_convert_fusion.5.refs_0_, ...), custom_call_target="tpu_custom_call" | custom-call | flops 4227858432 | bytes 11010048 | tf_op jit(solution)/shard_map/down/pallas_call | solution.py:253
  77.8 2.1 %collective-permute-start.24 = (bf16[384,512]{1,0:T(8,128)(2,1)S(1)}, bf16[384,512]{1,0:T(8,128)(2,1)S(1)}, u32[]{:S(2)}, u32[]{:S(2)}) collective-permute-start(bf16[384,512]{1,0:T(8,128)(2,1)S(1)} %add_convert_fusion.4.refs_0_), channel_id=1, source_target_pairs={{0,4},{1,5},{2,6},{3,7},{4,0},{5,1},{6,2},{7,3},{8,12},{9,13},{10,... | collective-permute-start | bytes 1179656 | tf_op jit(solution)/shard_map/ppermute | solution.py:38
  79.9 2.0 %down.13 = (bf16[384,512]{1,0:T(8,128)(2,1)S(1)}, f32[384,512]{1,0:T(8,128)S(1)}, bf16[1792,1024]{1,0:T(8,128)(2,1)S(1)}) custom-call(bf16[384,1792]{1,0:T(8,128)(2,1)S(1)} %get-tuple-element.96.hidden_ref, bf16[1792,1024]{1,0:T(8,128)(2,1)S(1)} %get-tuple-element.108.w_now, bf16[384,512]{1,0:T(8,128)(2,1)S(1)} %add_convert_fusion.4.refs_0_, ...), custom_call_target="tpu_custom_call" | custom-call | flops 4227858432 | bytes 11010048 | tf_op jit(solution)/shard_map/down/pallas_call | solution.py:253
  86.1 3.8 %collective-permute-done.24 = bf16[384,512]{1,0:T(8,128)(2,1)S(1)} collective-permute-done((bf16[384,512]{1,0:T(8,128)(2,1)S(1)}, bf16[384,512]{1,0:T(8,128)(2,1)S(1)}, u32[]{:S(2)}, u32[]{:S(2)}) %collective-permute-start.24) | collective-permute-done | bytes 393248 | tf_op jit(solution)/shard_map/ppermute | solution.py:38
  90.2 8.8 %collective-permute-start.29 = (bf16[384,512]{1,0:T(8,128)(2,1)S(1)}, bf16[384,512]{1,0:T(8,128)(2,1)S(1)}, u32[]{:S(2)}, u32[]{:S(2)}) collective-permute-start(bf16[384,512]{1,0:T(8,128)(2,1)S(1)} %add_convert_fusion.2.refs_0_), channel_id=1, source_target_pairs={{0,12},{1,13},{2,14},{3,15},{4,8},{5,9},{6,10},{7,11},{8,4},{9,5},... | collective-permute-start | bytes 1179656 | tf_op jit(solution)/shard_map/ppermute | solution.py:38
  102.6 6.4 %collective-permute-done.29 = bf16[384,512]{1,0:T(8,128)(2,1)S(1)} collective-permute-done((bf16[384,512]{1,0:T(8,128)(2,1)S(1)}, bf16[384,512]{1,0:T(8,128)(2,1)S(1)}, u32[]{:S(2)}, u32[]{:S(2)}) %collective-permute-start.29) | collective-permute-done | bytes 393248 | tf_op jit(solution)/shard_map/ppermute | solution.py:38
  109.0 6.5 %collective-permute-done.27 = bf16[384,512]{1,0:T(8,128)(2,1)S(1)} collective-permute-done((bf16[384,512]{1,0:T(8,128)(2,1)S(1)}, bf16[384,512]{1,0:T(8,128)(2,1)S(1)}, u32[]{:S(2)}, u32[]{:S(2)}) %collective-permute-start.27) | collective-permute-done | bytes 393248 | tf_op jit(solution)/shard_map/ppermute | solution.py:38
  (73 shorter events, 27.9 us)
Async XLA Ops:
  2.0 12.5 %collective-permute-start.1 = (bf16[400,512]{1,0:T(8,128)(2,1)S(1)}, bf16[400,512]{1,0:T(8,128)(2,1)S(1)}, u32[]{:S(2)}, u32[]{:S(2)}) collective-permute-start(bf16[400,512]{1,0:T(8,128)(2,1)S(1)} %pad_maximum_fusion.mine), channel_id=1, source_target_pairs={{0,2},{1,3},{2,0},{3,1},{4,6},{5,7},{6,4},{7,5},{8,10},{9,11},{10,... | collective-permute-start | bytes 1228808 | tf_op jit(solution)/shard_map/ppermute | solution.py:38
  5.0 9.5 %collective-permute-start.3 = (bf16[400,512]{1,0:T(8,128)(2,1)S(1)}, bf16[400,512]{1,0:T(8,128)(2,1)S(1)}, u32[]{:S(2)}, u32[]{:S(2)}) collective-permute-start(bf16[400,512]{1,0:T(8,128)(2,1)S(1)} %pad_maximum_fusion.mine), channel_id=1, source_target_pairs={{0,1},{1,0},{2,3},{3,2},{4,5},{5,4},{6,7},{7,6},{8,9},{9,8},{10,11... | collective-permute-start | bytes 1228808 | tf_op jit(solution)/shard_map/ppermute | solution.py:38
  5.0 13.7 %collective-permute-start.5 = (bf16[400,512]{1,0:T(8,128)(2,1)S(1)}, bf16[400,512]{1,0:T(8,128)(2,1)S(1)}, u32[]{:S(2)}, u32[]{:S(2)}) collective-permute-start(bf16[400,512]{1,0:T(8,128)(2,1)S(1)} %pad_maximum_fusion.mine), channel_id=1, source_target_pairs={{0,4},{1,5},{2,6},{3,7},{4,0},{5,1},{6,2},{7,3},{8,12},{9,13},{10,... | collective-permute-start | bytes 1228808 | tf_op jit(solution)/shard_map/ppermute | solution.py:38
  6.6 21.2 %collective-permute-start = (bf16[400,512]{1,0:T(8,128)(2,1)S(1)}, bf16[400,512]{1,0:T(8,128)(2,1)S(1)}, u32[]{:S(2)}, u32[]{:S(2)}) collective-permute-start(bf16[400,512]{1,0:T(8,128)(2,1)S(1)} %pad_maximum_fusion.mine), channel_id=1, source_target_pairs={{0,12},{1,13},{2,14},{3,15},{4,8},{5,9},{6,10},{7,11},{8,4},{9,5},... | collective-permute-start | bytes 1228808 | tf_op jit(solution)/shard_map/ppermute | solution.py:38
  14.4 6.5 %collective-permute-start.2 = (bf16[400,512]{1,0:T(8,128)(2,1)S(1)}, bf16[400,512]{1,0:T(8,128)(2,1)S(1)}, u32[]{:S(2)}, u32[]{:S(2)}) collective-permute-start(bf16[400,512]{1,0:T(8,128)(2,1)S(1)} %collective-permute-done.1.mine), channel_id=1, source_target_pairs={{0,1},{1,0},{2,3},{3,2},{4,5},{5,4},{6,7},{7,6},{8,9},{9,8},{10,11... | collective-permute-start | bytes 1228808 | tf_op jit(solution)/shard_map/ppermute | solution.py:38
  18.7 12.1 %collective-permute-start.8 = (bf16[400,512]{1,0:T(8,128)(2,1)S(1)}, bf16[400,512]{1,0:T(8,128)(2,1)S(1)}, u32[]{:S(2)}, u32[]{:S(2)}) collective-permute-start(bf16[400,512]{1,0:T(8,128)(2,1)S(1)} %constant_dynamic-update-slice_fusion.2.mine), channel_id=1, source_target_pairs={{0,1},{1,0},{2,3},{3,2},{4,5},{5,4},{6,7},{7,6},{8,9},{9,8},{10,11... | collective-permute-start | bytes 1228808 | tf_op jit(solution)/shard_map/ppermute | solution.py:38
  19.2 11.6 %collective-permute-start.6 = (bf16[400,512]{1,0:T(8,128)(2,1)S(1)}, bf16[400,512]{1,0:T(8,128)(2,1)S(1)}, u32[]{:S(2)}, u32[]{:S(2)}) collective-permute-start(bf16[400,512]{1,0:T(8,128)(2,1)S(1)} %constant_dynamic-update-slice_fusion.2.mine), channel_id=1, source_target_pairs={{0,2},{1,3},{2,0},{3,1},{4,6},{5,7},{6,4},{7,5},{8,10},{9,11},{10,... | collective-permute-start | bytes 1228808 | tf_op jit(solution)/shard_map/ppermute | solution.py:38
  27.8 14.5 %collective-permute-start.12 = (bf16[400,512]{1,0:T(8,128)(2,1)S(1)}, bf16[400,512]{1,0:T(8,128)(2,1)S(1)}, u32[]{:S(2)}, u32[]{:S(2)}) collective-permute-start(bf16[400,512]{1,0:T(8,128)(2,1)S(1)} %constant_dynamic-update-slice_fusion.3.mine), channel_id=1, source_target_pairs={{0,1},{1,0},{2,3},{3,2},{4,5},{5,4},{6,7},{7,6},{8,9},{9,8},{10,11... | collective-permute-start | bytes 1228808 | tf_op jit(solution)/shard_map/ppermute | solution.py:38
  27.8 14.5 %collective-permute-start.10 = (bf16[400,512]{1,0:T(8,128)(2,1)S(1)}, bf16[400,512]{1,0:T(8,128)(2,1)S(1)}, u32[]{:S(2)}, u32[]{:S(2)}) collective-permute-start(bf16[400,512]{1,0:T(8,128)(2,1)S(1)} %constant_dynamic-update-slice_fusion.3.mine), channel_id=1, source_target_pairs={{0,2},{1,3},{2,0},{3,1},{4,6},{5,7},{6,4},{7,5},{8,10},{9,11},{10,... | collective-permute-start | bytes 1228808 | tf_op jit(solution)/shard_map/ppermute | solution.py:38
  28.3 11.6 %collective-permute-start.4 = (bf16[400,512]{1,0:T(8,128)(2,1)S(1)}, bf16[400,512]{1,0:T(8,128)(2,1)S(1)}, u32[]{:S(2)}, u32[]{:S(2)}) collective-permute-start(bf16[400,512]{1,0:T(8,128)(2,1)S(1)} %constant_dynamic-update-slice_fusion.3.mine), channel_id=1, source_target_pairs={{0,4},{1,5},{2,6},{3,7},{4,0},{5,1},{6,2},{7,3},{8,12},{9,13},{10,... | collective-permute-start | bytes 1228808 | tf_op jit(solution)/shard_map/ppermute | solution.py:38
  39.9 12.1 %collective-permute-start.14 = (bf16[400,512]{1,0:T(8,128)(2,1)S(1)}, bf16[400,512]{1,0:T(8,128)(2,1)S(1)}, u32[]{:S(2)}, u32[]{:S(2)}) collective-permute-start(bf16[400,512]{1,0:T(8,128)(2,1)S(1)} %constant_dynamic-update-slice_fusion.1.mine), channel_id=1, source_target_pairs={{0,1},{1,0},{2,3},{3,2},{4,5},{5,4},{6,7},{7,6},{8,9},{9,8},{10,11... | collective-permute-start | bytes 1228808 | tf_op jit(solution)/shard_map/ppermute | solution.py:38
  39.9 12.1 %collective-permute-start.9 = (bf16[400,512]{1,0:T(8,128)(2,1)S(1)}, bf16[400,512]{1,0:T(8,128)(2,1)S(1)}, u32[]{:S(2)}, u32[]{:S(2)}) collective-permute-start(bf16[400,512]{1,0:T(8,128)(2,1)S(1)} %constant_dynamic-update-slice_fusion.1.mine), channel_id=1, source_target_pairs={{0,2},{1,3},{2,0},{3,1},{4,6},{5,7},{6,4},{7,5},{8,10},{9,11},{10,... | collective-permute-start | bytes 1228808 | tf_op jit(solution)/shard_map/ppermute | solution.py:38
  42.3 4.2 %collective-permute-start.11 = (bf16[400,512]{1,0:T(8,128)(2,1)S(1)}, bf16[400,512]{1,0:T(8,128)(2,1)S(1)}, u32[]{:S(2)}, u32[]{:S(2)}) collective-permute-start(bf16[400,512]{1,0:T(8,128)(2,1)S(1)} %collective-permute-done.10.mine), channel_id=1, source_target_pairs={{0,1},{1,0},{2,3},{3,2},{4,5},{5,4},{6,7},{7,6},{8,9},{9,8},{10,11... | collective-permute-start | bytes 1228808 | tf_op jit(solution)/shard_map/ppermute | solution.py:38
  52.0 4.2 %collective-permute-start.13 = (bf16[400,512]{1,0:T(8,128)(2,1)S(1)}, bf16[400,512]{1,0:T(8,128)(2,1)S(1)}, u32[]{:S(2)}, u32[]{:S(2)}) collective-permute-start(bf16[400,512]{1,0:T(8,128)(2,1)S(1)} %constant_dynamic-update-slice_fusion.mine), channel_id=1, source_target_pairs={{0,1},{1,0},{2,3},{3,2},{4,5},{5,4},{6,7},{7,6},{8,9},{9,8},{10,11... | collective-permute-start | bytes 1228808 | tf_op jit(solution)/shard_map/ppermute | solution.py:38
  65.6 4.4 %collective-permute-start.16 = (bf16[384,512]{1,0:T(8,128)(2,1)S(1)}, bf16[384,512]{1,0:T(8,128)(2,1)S(1)}, u32[]{:S(2)}, u32[]{:S(2)}) collective-permute-start(bf16[384,512]{1,0:T(8,128)(2,1)S(1)} %get-tuple-element.104), channel_id=1, source_target_pairs={{0,1},{1,0},{2,3},{3,2},{4,5},{5,4},{6,7},{7,6},{8,9},{9,8},{10,11... | collective-permute-start | bytes 1179656 | tf_op jit(solution)/shard_map/ppermute | solution.py:38
  65.9 11.7 %collective-permute-start.19 = (bf16[384,512]{1,0:T(8,128)(2,1)S(1)}, bf16[384,512]{1,0:T(8,128)(2,1)S(1)}, u32[]{:S(2)}, u32[]{:S(2)}) collective-permute-start(bf16[384,512]{1,0:T(8,128)(2,1)S(1)} %add_convert_fusion.7.refs_0_), channel_id=1, source_target_pairs={{0,2},{1,3},{2,0},{3,1},{4,6},{5,7},{6,4},{7,5},{8,10},{9,11},{10,... | collective-permute-start | bytes 1179656 | tf_op jit(solution)/shard_map/ppermute | solution.py:38
  70.1 12.0 %collective-permute-start.21 = (bf16[384,512]{1,0:T(8,128)(2,1)S(1)}, bf16[384,512]{1,0:T(8,128)(2,1)S(1)}, u32[]{:S(2)}, u32[]{:S(2)}) collective-permute-start(bf16[384,512]{1,0:T(8,128)(2,1)S(1)} %add_convert_fusion.6.refs_0_), channel_id=1, source_target_pairs={{0,4},{1,5},{2,6},{3,7},{4,0},{5,1},{6,2},{7,3},{8,12},{9,13},{10,... | collective-permute-start | bytes 1179656 | tf_op jit(solution)/shard_map/ppermute | solution.py:38
  74.1 12.1 %collective-permute-start.23 = (bf16[384,512]{1,0:T(8,128)(2,1)S(1)}, bf16[384,512]{1,0:T(8,128)(2,1)S(1)}, u32[]{:S(2)}, u32[]{:S(2)}) collective-permute-start(bf16[384,512]{1,0:T(8,128)(2,1)S(1)} %add_convert_fusion.5.refs_0_), channel_id=1, source_target_pairs={{0,2},{1,3},{2,0},{3,1},{4,6},{5,7},{6,4},{7,5},{8,10},{9,11},{10,... | collective-permute-start | bytes 1179656 | tf_op jit(solution)/shard_map/ppermute | solution.py:38
  76.7 5.4 %collective-permute-start.20 = (bf16[384,512]{1,0:T(8,128)(2,1)S(1)}, bf16[384,512]{1,0:T(8,128)(2,1)S(1)}, u32[]{:S(2)}, u32[]{:S(2)}) collective-permute-start(bf16[384,512]{1,0:T(8,128)(2,1)S(1)} %get-tuple-element.113), channel_id=1, source_target_pairs={{0,1},{1,0},{2,3},{3,2},{4,5},{5,4},{6,7},{7,6},{8,9},{9,8},{10,11... | collective-permute-start | bytes 1179656 | tf_op jit(solution)/shard_map/ppermute | solution.py:38
  77.8 12.2 %collective-permute-start.24 = (bf16[384,512]{1,0:T(8,128)(2,1)S(1)}, bf16[384,512]{1,0:T(8,128)(2,1)S(1)}, u32[]{:S(2)}, u32[]{:S(2)}) collective-permute-start(bf16[384,512]{1,0:T(8,128)(2,1)S(1)} %add_convert_fusion.4.refs_0_), channel_id=1, source_target_pairs={{0,4},{1,5},{2,6},{3,7},{4,0},{5,1},{6,2},{7,3},{8,12},{9,13},{10,... | collective-permute-start | bytes 1179656 | tf_op jit(solution)/shard_map/ppermute | solution.py:38
  82.3 20.3 %collective-permute-start.28 = (bf16[384,512]{1,0:T(8,128)(2,1)S(1)}, bf16[384,512]{1,0:T(8,128)(2,1)S(1)}, u32[]{:S(2)}, u32[]{:S(2)}) collective-permute-start(bf16[384,512]{1,0:T(8,128)(2,1)S(1)} %add_convert_fusion.3.refs_0_), channel_id=1, source_target_pairs={{0,2},{1,3},{2,0},{3,1},{4,6},{5,7},{6,4},{7,5},{8,10},{9,11},{10,... | collective-permute-start | bytes 1179656 | tf_op jit(solution)/shard_map/ppermute | solution.py:38
  85.9 15.0 %collective-permute-start.26 = (bf16[384,512]{1,0:T(8,128)(2,1)S(1)}, bf16[384,512]{1,0:T(8,128)(2,1)S(1)}, u32[]{:S(2)}, u32[]{:S(2)}) collective-permute-start(bf16[384,512]{1,0:T(8,128)(2,1)S(1)} %get-tuple-element.120), channel_id=1, source_target_pairs={{0,1},{1,0},{2,3},{3,2},{4,5},{5,4},{6,7},{7,6},{8,9},{9,8},{10,11... | collective-permute-start | bytes 1179656 | tf_op jit(solution)/shard_map/ppermute | solution.py:38
  90.2 18.8 %collective-permute-start.29 = (bf16[384,512]{1,0:T(8,128)(2,1)S(1)}, bf16[384,512]{1,0:T(8,128)(2,1)S(1)}, u32[]{:S(2)}, u32[]{:S(2)}) collective-permute-start(bf16[384,512]{1,0:T(8,128)(2,1)S(1)} %add_convert_fusion.2.refs_0_), channel_id=1, source_target_pairs={{0,12},{1,13},{2,14},{3,15},{4,8},{5,9},{6,10},{7,11},{8,4},{9,5},... | collective-permute-start | bytes 1179656 | tf_op jit(solution)/shard_map/ppermute | solution.py:38
  101.0 14.5 %collective-permute-start.27 = (bf16[384,512]{1,0:T(8,128)(2,1)S(1)}, bf16[384,512]{1,0:T(8,128)(2,1)S(1)}, u32[]{:S(2)}, u32[]{:S(2)}) collective-permute-start(bf16[384,512]{1,0:T(8,128)(2,1)S(1)} %add_convert_fusion.1), channel_id=1, source_target_pairs={{0,4},{1,5},{2,6},{3,7},{4,0},{5,1},{6,2},{7,3},{8,12},{9,13},{10,... | collective-permute-start | bytes 1179656 | tf_op jit(solution)/shard_map/ppermute | solution.py:38
  (6 other events, 20.2 us)

commit v4 on v3

--- a/solution.py
+++ b/solution.py
@@ -115,7 +115,7 @@
             ref[...] = jnp.zeros_like(ref)
     units = hidden_ref.shape[1] if last else gate_out.shape[1]
     def block(n, _):
-        cols = pl.ds(pl.multiple_of(n * COLS, COLS), COLS)
+        cols = pl.ds(n * COLS if isinstance(n, int) else pl.multiple_of(n * COLS, COLS), COLS)
         gate = jnp.dot(both[...], w_now[0, :, cols], preferred_element_type=jnp.float32)
         up = jnp.dot(both[...], w_now[1, :, cols], preferred_element_type=jnp.float32)
         if not first:
@@ -130,7 +130,13 @@
             up_out[:, cols] = up
         return 0
 
-    lax.fori_loop(0, units // COLS, block, 0)
+    def two_blocks(n, _):
+        return block(2 * n + 1, block(2 * n, 0))
+
+    blocks = units // COLS
+    lax.fori_loop(0, blocks // 2, two_blocks, 0)
+    if blocks % 2:
+        block(blocks - 1, 0)
     landed(copies)
 
 

time: 117 us -> 115 us (0.983)
  waiting for transfers between devices: 27.2 us -> 33.3 us
  starting transfers between devices: 31.1 us -> 26.6 us
  Pallas kernels: 53.9 us -> 50.7 us
    ppermute x30, waiting for transfers between devices: 27.2 us -> 33.3 us  [swap(): lax.ppermute(value, AXIS, [(i, i ^ mask) for i in range(lax.axis_size(AXI...]
    ppermute x30, starting transfers between devices: 31.1 us -> 26.6 us  [swap(): lax.ppermute(value, AXIS, [(i, i ^ mask) for i in range(lax.axis_size(AXI...]
    pallas_call x8, Pallas kernels: 34 us -> 30.8 us  [gate_up(): pl.pallas_call(functools.partial(gate_up_kernel, features, first, last, a...]
  transfers between devices with their start and end apart: 30 -> 30, of which waited for: 11 -> 12; matrix products, arithmetic and copies ran while one was open for 1% -> 1% of each run, Pallas kernels for 40% -> 39%
where the time goes in v4:
time: 115 us
  Pallas kernels  50.7 us (44%)
  waiting for transfers between devices  33.3 us (29%)
  starting transfers between devices  26.6 us (23%)
  other arithmetic  3.94 us (3%)
    ppermute x30, waiting for transfers between devices, swap(): lax.ppermute(value, AXIS, [(i, i ^ mask) for i in range(lax.axis_size(AXI...  33.3 us
    pallas_call x8, Pallas kernels, gate_up(): pl.pallas_call(functools.partial(gate_up_kernel, features, first, last, a...  30.8 us
    ppermute x30, starting transfers between devices, swap(): lax.ppermute(value, AXIS, [(i, i ^ mask) for i in range(lax.axis_size(AXI...  26.6 us
    pallas_call x8, Pallas kernels, down(): pl.pallas_call(functools.partial(down_kernel, last, len(after), ahead), i...  16.1 us
    pallas_call x1, Pallas kernels, first_fetch(): pl.pallas_call(first_fetch_kernel, in_specs=[in_hbm(), in_hbm()], out_spe...  3.77 us
  transfers between devices with their start and end apart: 30, of which 12 were waited for; matrix products, arithmetic and copies ran while one was open for 1% of the time, Pallas kernels for 39%

profile of v4, /device:TPU:0, one launch (start us, length us, event | category | flops | bytes accessed | tf_op | source)
XLA Modules:
  0.0 114.9 jit_solution(15402417413472362421)
XLA Ops:
  2.0 3.0 %collective-permute-start.1 = (bf16[400,512]{1,0:T(8,128)(2,1)S(1)}, bf16[400,512]{1,0:T(8,128)(2,1)S(1)}, u32[]{:S(2)}, u32[]{:S(2)}) collective-permute-start(bf16[400,512]{1,0:T(8,128)(2,1)S(1)} %pad_maximum_fusion.mine), channel_id=1, source_target_pairs={{0,2},{1,3},{2,0},{3,1},{4,6},{5,7},{6,4},{7,5},{8,10},{9,11},{10,... | collective-permute-start | bytes 1228808 | tf_op jit(solution)/shard_map/ppermute | solution.py:38
  6.6 2.5 %collective-permute-start = (bf16[400,512]{1,0:T(8,128)(2,1)S(1)}, bf16[400,512]{1,0:T(8,128)(2,1)S(1)}, u32[]{:S(2)}, u32[]{:S(2)}) collective-permute-start(bf16[400,512]{1,0:T(8,128)(2,1)S(1)} %pad_maximum_fusion.mine), channel_id=1, source_target_pairs={{0,12},{1,13},{2,14},{3,15},{4,8},{5,9},{6,10},{7,11},{8,4},{9,5},... | collective-permute-start | bytes 1228808 | tf_op jit(solution)/shard_map/ppermute | solution.py:38
  9.0 3.8 %first_fetch.1 = (bf16[8,512]{1,0:T(8,128)(2,1)}, bf16[2,1024,1792]{2,1,0:T(8,128)(2,1)S(1)}) custom-call(bf16[8192,1792]{1,0:T(8,128)(2,1)} %refs_4_.12, bf16[8192,1792]{1,0:T(8,128)(2,1)} %refs_5_.11), custom_call_target="tpu_custom_call" | custom-call | bytes 29360128 | tf_op jit(solution)/shard_map/first_fetch/pallas_call | solution.py:169
  14.4 3.6 %gate_up.8 = (f32[384,1792]{1,0:T(8,128)S(1)}, f32[384,1792]{1,0:T(8,128)S(1)}, f32[1,384]{1,0:T(1,128)S(1)}, bf16[8,512]{1,0:T(8,128)(2,1)S(1)}, bf16[2,1024,1792]{2,1,0:T(8,128)(2,1)S(1)}) custom-call(bf16[400,512]{1,0:T(8,128)(2,1)S(1)} %pad_maximum_fusion.mine, bf16[400,512]{1,0:T(8,128)(2,1)S(1)} %collective-permute-done.3.other, ...), custom_call_target="tpu_custom_call" | custom-call | flops 5637144576 | bytes 14680064 | tf_op jit(solution)/shard_map/gate_up/pallas_call | solution.py:207
  20.4 3.8 %gate_up.9 = (f32[384,1792]{1,0:T(8,128)S(1)}, f32[384,1792]{1,0:T(8,128)S(1)}, f32[1,384]{1,0:T(1,128)S(1)}, bf16[8,512]{1,0:T(8,128)(2,1)S(1)}, bf16[2,1024,1792]{2,1,0:T(8,128)(2,1)S(1)}) custom-call(bf16[400,512]{1,0:T(8,128)(2,1)S(1)} %collective-permute-done.1.mine, ...), custom_call_target="tpu_custom_call", output_to_operand_aliasing={{0}: (3, {}), {1}: (4, {}), {2}: (5, {})} | custom-call | flops 5637144576 | bytes 14680064 | tf_op jit(solution)/shard_map/gate_up/pallas_call | solution.py:207
  24.2 3.5 %collective-permute-done = bf16[400,512]{1,0:T(8,128)(2,1)S(1)} collective-permute-done((bf16[400,512]{1,0:T(8,128)(2,1)S(1)}, bf16[400,512]{1,0:T(8,128)(2,1)S(1)}, u32[]{:S(2)}, u32[]{:S(2)}) %collective-permute-start) | collective-permute-done | bytes 409632 | tf_op jit(solution)/shard_map/ppermute | solution.py:38
  30.1 3.8 %gate_up.10 = (f32[384,1792]{1,0:T(8,128)S(1)}, f32[384,1792]{1,0:T(8,128)S(1)}, f32[1,384]{1,0:T(1,128)S(1)}, bf16[2,1024,1792]{2,1,0:T(8,128)(2,1)S(1)}) custom-call(bf16[400,512]{1,0:T(8,128)(2,1)S(1)} %constant_dynamic-update-slice_fusion.2.mine, ...), custom_call_target="tpu_custom_call", output_to_operand_aliasing={{0}: (3, {}), {1}: (4, {}), {2}: (5, {})} | custom-call | flops 5637144576 | bytes 14680064 | tf_op jit(solution)/shard_map/gate_up/pallas_call | solution.py:207
  34.0 3.8 %gate_up.11 = (f32[384,1792]{1,0:T(8,128)S(1)}, f32[384,1792]{1,0:T(8,128)S(1)}, f32[1,384]{1,0:T(1,128)S(1)}, bf16[8,512]{1,0:T(8,128)(2,1)S(1)}, bf16[2,1024,1792]{2,1,0:T(8,128)(2,1)S(1)}) custom-call(bf16[400,512]{1,0:T(8,128)(2,1)S(1)} %collective-permute-done.6.mine, ...), custom_call_target="tpu_custom_call", output_to_operand_aliasing={{0}: (3, {}), {1}: (4, {}), {2}: (5, {})} | custom-call | flops 5637144576 | bytes 14680064 | tf_op jit(solution)/shard_map/gate_up/pallas_call | solution.py:207
  37.8 2.1 %collective-permute-done.4 = bf16[400,512]{1,0:T(8,128)(2,1)S(1)} collective-permute-done((bf16[400,512]{1,0:T(8,128)(2,1)S(1)}, bf16[400,512]{1,0:T(8,128)(2,1)S(1)}, u32[]{:S(2)}, u32[]{:S(2)}) %collective-permute-start.4) | collective-permute-done | bytes 409632 | tf_op jit(solution)/shard_map/ppermute | solution.py:38
  41.6 3.8 %gate_up.12 = (f32[384,1792]{1,0:T(8,128)S(1)}, f32[384,1792]{1,0:T(8,128)S(1)}, f32[1,384]{1,0:T(1,128)S(1)}, bf16[2,1024,1792]{2,1,0:T(8,128)(2,1)S(1)}) custom-call(bf16[400,512]{1,0:T(8,128)(2,1)S(1)} %constant_dynamic-update-slice_fusion.3.mine, ...), custom_call_target="tpu_custom_call", output_to_operand_aliasing={{0}: (3, {}), {1}: (4, {}), {2}: (5, {})} | custom-call | flops 5637144576 | bytes 14680064 | tf_op jit(solution)/shard_map/gate_up/pallas_call | solution.py:207
  45.5 3.8 %gate_up.13 = (f32[384,1792]{1,0:T(8,128)S(1)}, f32[384,1792]{1,0:T(8,128)S(1)}, f32[1,384]{1,0:T(1,128)S(1)}, bf16[8,512]{1,0:T(8,128)(2,1)S(1)}, bf16[2,1024,1792]{2,1,0:T(8,128)(2,1)S(1)}) custom-call(bf16[400,512]{1,0:T(8,128)(2,1)S(1)} %collective-permute-done.10.mine, ...), custom_call_target="tpu_custom_call", output_to_operand_aliasing={{0}: (3, {}), {1}: (4, {}), {2}: (5, {})} | custom-call | flops 5637144576 | bytes 14680064 | tf_op jit(solution)/shard_map/gate_up/pallas_call | solution.py:207
  49.3 2.5 %collective-permute-done.9 = bf16[400,512]{1,0:T(8,128)(2,1)S(1)} collective-permute-done((bf16[400,512]{1,0:T(8,128)(2,1)S(1)}, bf16[400,512]{1,0:T(8,128)(2,1)S(1)}, u32[]{:S(2)}, u32[]{:S(2)}) %collective-permute-start.9) | collective-permute-done | bytes 409632 | tf_op jit(solution)/shard_map/ppermute | solution.py:38
  51.8 3.8 %gate_up.14 = (f32[384,1792]{1,0:T(8,128)S(1)}, f32[384,1792]{1,0:T(8,128)S(1)}, f32[1,384]{1,0:T(1,128)S(1)}, bf16[2,1024,1792]{2,1,0:T(8,128)(2,1)S(1)}) custom-call(bf16[400,512]{1,0:T(8,128)(2,1)S(1)} %constant_dynamic-update-slice_fusion.1.mine, ...), custom_call_target="tpu_custom_call", output_to_operand_aliasing={{0}: (3, {}), {1}: (4, {}), {2}: (5, {})} | custom-call | flops 5637144576 | bytes 14680064 | tf_op jit(solution)/shard_map/gate_up/pallas_call | solution.py:207
  55.6 4.3 %gate_up.15 = (bf16[384,1792]{1,0:T(8,128)(2,1)S(1)}, bf16[1792,1024]{1,0:T(8,128)(2,1)S(1)}) custom-call(bf16[400,512]{1,0:T(8,128)(2,1)S(1)} %constant_dynamic-update-slice_fusion.mine, bf16[400,512]{1,0:T(8,128)(2,1)S(1)} %collective-permute-done.13.other, bf16[2,1024,1792]{2,1,0:T(8,128)(2,1)S(1)} %get-tuple-element.92.refs_0_, ...), custom_call_target="tpu_custom_call" | custom-call | flops 5637144576 | bytes 14680064 | tf_op jit(solution)/shard_map/gate_up/pallas_call | solution.py:207
  59.9 2.1 %down.8 = (bf16[384,512]{1,0:T(8,128)(2,1)S(1)}, f32[384,512]{1,0:T(8,128)S(1)}, bf16[1792,1024]{1,0:T(8,128)(2,1)S(1)}) custom-call(bf16[384,1792]{1,0:T(8,128)(2,1)S(1)} %get-tuple-element.96.hidden_ref, bf16[1792,1024]{1,0:T(8,128)(2,1)S(1)} %get-tuple-element.97.w_now, bf16[1792,8192]{1,0:T(8,128)(2,1)} %refs_1_.11), custom_call_target="tpu_custom_call" | custom-call | flops 4227858432 | bytes 11010048 | tf_op jit(solution)/shard_map/down/pallas_call | solution.py:259
  62.5 2.0 %down.9 = (bf16[384,512]{1,0:T(8,128)(2,1)S(1)}, f32[384,512]{1,0:T(8,128)S(1)}, bf16[1792,1024]{1,0:T(8,128)(2,1)S(1)}) custom-call(bf16[384,1792]{1,0:T(8,128)(2,1)S(1)} %get-tuple-element.96.hidden_ref, bf16[1792,1024]{1,0:T(8,128)(2,1)S(1)} %get-tuple-element.98.w_now, bf16[1792,8192]{1,0:T(8,128)(2,1)} %refs_1_.11), custom_call_target="tpu_custom_call" | custom-call | flops 4227858432 | bytes 11010048 | tf_op jit(solution)/shard_map/down/pallas_call | solution.py:259
  66.4 2.0 %down.10 = (bf16[384,512]{1,0:T(8,128)(2,1)S(1)}, f32[384,512]{1,0:T(8,128)S(1)}, bf16[1792,1024]{1,0:T(8,128)(2,1)S(1)}) custom-call(bf16[384,1792]{1,0:T(8,128)(2,1)S(1)} %get-tuple-element.96.hidden_ref, bf16[1792,1024]{1,0:T(8,128)(2,1)S(1)} %get-tuple-element.99.w_now, bf16[384,512]{1,0:T(8,128)(2,1)S(1)} %add_convert_fusion.7.refs_0_, ...), custom_call_target="tpu_custom_call" | custom-call | flops 4227858432 | bytes 11010048 | tf_op jit(solution)/shard_map/down/pallas_call | solution.py:259
  69.7 2.0 %down.11 = (bf16[384,512]{1,0:T(8,128)(2,1)S(1)}, f32[384,512]{1,0:T(8,128)S(1)}, bf16[1792,1024]{1,0:T(8,128)(2,1)S(1)}) custom-call(bf16[384,1792]{1,0:T(8,128)(2,1)S(1)} %get-tuple-element.96.hidden_ref, bf16[1792,1024]{1,0:T(8,128)(2,1)S(1)} %get-tuple-element.102.w_now, bf16[384,512]{1,0:T(8,128)(2,1)S(1)} %add_convert_fusion.6.refs_0_, ...), custom_call_target="tpu_custom_call" | custom-call | flops 4227858432 | bytes 11010048 | tf_op jit(solution)/shard_map/down/pallas_call | solution.py:259
  74.7 2.1 %collective-permute-done.19 = bf16[384,512]{1,0:T(8,128)(2,1)S(1)} collective-permute-done((bf16[384,512]{1,0:T(8,128)(2,1)S(1)}, bf16[384,512]{1,0:T(8,128)(2,1)S(1)}, u32[]{:S(2)}, u32[]{:S(2)}) %collective-permute-start.19) | collective-permute-done | bytes 393248 | tf_op jit(solution)/shard_map/ppermute | solution.py:38
  81.7 2.0 %down.14 = (bf16[384,512]{1,0:T(8,128)(2,1)S(1)}, f32[384,512]{1,0:T(8,128)S(1)}, bf16[1792,1024]{1,0:T(8,128)(2,1)S(1)}) custom-call(bf16[384,1792]{1,0:T(8,128)(2,1)S(1)} %get-tuple-element.96.hidden_ref, bf16[1792,1024]{1,0:T(8,128)(2,1)S(1)} %get-tuple-element.111.w_now, bf16[384,512]{1,0:T(8,128)(2,1)S(1)} %add_convert_fusion.3.refs_0_, ...), custom_call_target="tpu_custom_call" | custom-call | flops 4227858432 | bytes 11010048 | tf_op jit(solution)/shard_map/down/pallas_call | solution.py:259
  85.2 3.4 %collective-permute-done.24 = bf16[384,512]{1,0:T(8,128)(2,1)S(1)} collective-permute-done((bf16[384,512]{1,0:T(8,128)(2,1)S(1)}, bf16[384,512]{1,0:T(8,128)(2,1)S(1)}, u32[]{:S(2)}, u32[]{:S(2)}) %collective-permute-start.24) | collective-permute-done | bytes 393248 | tf_op jit(solution)/shard_map/ppermute | solution.py:38
  88.9 8.5 %collective-permute-start.29 = (bf16[384,512]{1,0:T(8,128)(2,1)S(1)}, bf16[384,512]{1,0:T(8,128)(2,1)S(1)}, u32[]{:S(2)}, u32[]{:S(2)}) collective-permute-start(bf16[384,512]{1,0:T(8,128)(2,1)S(1)} %add_convert_fusion.2.refs_0_), channel_id=1, source_target_pairs={{0,12},{1,13},{2,14},{3,15},{4,8},{5,9},{6,10},{7,11},{8,4},{9,5},... | collective-permute-start | bytes 1179656 | tf_op jit(solution)/shard_map/ppermute | solution.py:38
  101.0 6.4 %collective-permute-done.29 = bf16[384,512]{1,0:T(8,128)(2,1)S(1)} collective-permute-done((bf16[384,512]{1,0:T(8,128)(2,1)S(1)}, bf16[384,512]{1,0:T(8,128)(2,1)S(1)}, u32[]{:S(2)}, u32[]{:S(2)}) %collective-permute-start.29) | collective-permute-done | bytes 393248 | tf_op jit(solution)/shard_map/ppermute | solution.py:38
  107.4 6.5 %collective-permute-done.27 = bf16[384,512]{1,0:T(8,128)(2,1)S(1)} collective-permute-done((bf16[384,512]{1,0:T(8,128)(2,1)S(1)}, bf16[384,512]{1,0:T(8,128)(2,1)S(1)}, u32[]{:S(2)}, u32[]{:S(2)}) %collective-permute-start.27) | collective-permute-done | bytes 393248 | tf_op jit(solution)/shard_map/ppermute | solution.py:38
  (73 shorter events, 29.2 us)
Async XLA Ops:
  2.0 12.5 %collective-permute-start.1 = (bf16[400,512]{1,0:T(8,128)(2,1)S(1)}, bf16[400,512]{1,0:T(8,128)(2,1)S(1)}, u32[]{:S(2)}, u32[]{:S(2)}) collective-permute-start(bf16[400,512]{1,0:T(8,128)(2,1)S(1)} %pad_maximum_fusion.mine), channel_id=1, source_target_pairs={{0,2},{1,3},{2,0},{3,1},{4,6},{5,7},{6,4},{7,5},{8,10},{9,11},{10,... | collective-permute-start | bytes 1228808 | tf_op jit(solution)/shard_map/ppermute | solution.py:38
  5.0 9.5 %collective-permute-start.3 = (bf16[400,512]{1,0:T(8,128)(2,1)S(1)}, bf16[400,512]{1,0:T(8,128)(2,1)S(1)}, u32[]{:S(2)}, u32[]{:S(2)}) collective-permute-start(bf16[400,512]{1,0:T(8,128)(2,1)S(1)} %pad_maximum_fusion.mine), channel_id=1, source_target_pairs={{0,1},{1,0},{2,3},{3,2},{4,5},{5,4},{6,7},{7,6},{8,9},{9,8},{10,11... | collective-permute-start | bytes 1228808 | tf_op jit(solution)/shard_map/ppermute | solution.py:38
  5.0 13.1 %collective-permute-start.5 = (bf16[400,512]{1,0:T(8,128)(2,1)S(1)}, bf16[400,512]{1,0:T(8,128)(2,1)S(1)}, u32[]{:S(2)}, u32[]{:S(2)}) collective-permute-start(bf16[400,512]{1,0:T(8,128)(2,1)S(1)} %pad_maximum_fusion.mine), channel_id=1, source_target_pairs={{0,4},{1,5},{2,6},{3,7},{4,0},{5,1},{6,2},{7,3},{8,12},{9,13},{10,... | collective-permute-start | bytes 1228808 | tf_op jit(solution)/shard_map/ppermute | solution.py:38
  6.6 21.2 %collective-permute-start = (bf16[400,512]{1,0:T(8,128)(2,1)S(1)}, bf16[400,512]{1,0:T(8,128)(2,1)S(1)}, u32[]{:S(2)}, u32[]{:S(2)}) collective-permute-start(bf16[400,512]{1,0:T(8,128)(2,1)S(1)} %pad_maximum_fusion.mine), channel_id=1, source_target_pairs={{0,12},{1,13},{2,14},{3,15},{4,8},{5,9},{6,10},{7,11},{8,4},{9,5},... | collective-permute-start | bytes 1228808 | tf_op jit(solution)/shard_map/ppermute | solution.py:38
  14.4 6.0 %collective-permute-start.2 = (bf16[400,512]{1,0:T(8,128)(2,1)S(1)}, bf16[400,512]{1,0:T(8,128)(2,1)S(1)}, u32[]{:S(2)}, u32[]{:S(2)}) collective-permute-start(bf16[400,512]{1,0:T(8,128)(2,1)S(1)} %collective-permute-done.1.mine), channel_id=1, source_target_pairs={{0,1},{1,0},{2,3},{3,2},{4,5},{5,4},{6,7},{7,6},{8,9},{9,8},{10,11... | collective-permute-start | bytes 1228808 | tf_op jit(solution)/shard_map/ppermute | solution.py:38
  18.1 12.0 %collective-permute-start.8 = (bf16[400,512]{1,0:T(8,128)(2,1)S(1)}, bf16[400,512]{1,0:T(8,128)(2,1)S(1)}, u32[]{:S(2)}, u32[]{:S(2)}) collective-permute-start(bf16[400,512]{1,0:T(8,128)(2,1)S(1)} %constant_dynamic-update-slice_fusion.2.mine), channel_id=1, source_target_pairs={{0,1},{1,0},{2,3},{3,2},{4,5},{5,4},{6,7},{7,6},{8,9},{9,8},{10,11... | collective-permute-start | bytes 1228808 | tf_op jit(solution)/shard_map/ppermute | solution.py:38
  18.7 11.5 %collective-permute-start.6 = (bf16[400,512]{1,0:T(8,128)(2,1)S(1)}, bf16[400,512]{1,0:T(8,128)(2,1)S(1)}, u32[]{:S(2)}, u32[]{:S(2)}) collective-permute-start(bf16[400,512]{1,0:T(8,128)(2,1)S(1)} %constant_dynamic-update-slice_fusion.2.mine), channel_id=1, source_target_pairs={{0,2},{1,3},{2,0},{3,1},{4,6},{5,7},{6,4},{7,5},{8,10},{9,11},{10,... | collective-permute-start | bytes 1228808 | tf_op jit(solution)/shard_map/ppermute | solution.py:38
  27.8 13.9 %collective-permute-start.12 = (bf16[400,512]{1,0:T(8,128)(2,1)S(1)}, bf16[400,512]{1,0:T(8,128)(2,1)S(1)}, u32[]{:S(2)}, u32[]{:S(2)}) collective-permute-start(bf16[400,512]{1,0:T(8,128)(2,1)S(1)} %constant_dynamic-update-slice_fusion.3.mine), channel_id=1, source_target_pairs={{0,1},{1,0},{2,3},{3,2},{4,5},{5,4},{6,7},{7,6},{8,9},{9,8},{10,11... | collective-permute-start | bytes 1228808 | tf_op jit(solution)/shard_map/ppermute | solution.py:38
  27.8 13.6 %collective-permute-start.10 = (bf16[400,512]{1,0:T(8,128)(2,1)S(1)}, bf16[400,512]{1,0:T(8,128)(2,1)S(1)}, u32[]{:S(2)}, u32[]{:S(2)}) collective-permute-start(bf16[400,512]{1,0:T(8,128)(2,1)S(1)} %constant_dynamic-update-slice_fusion.3.mine), channel_id=1, source_target_pairs={{0,2},{1,3},{2,0},{3,1},{4,6},{5,7},{6,4},{7,5},{8,10},{9,11},{10,... | collective-permute-start | bytes 1228808 | tf_op jit(solution)/shard_map/ppermute | solution.py:38
  28.3 11.6 %collective-permute-start.4 = (bf16[400,512]{1,0:T(8,128)(2,1)S(1)}, bf16[400,512]{1,0:T(8,128)(2,1)S(1)}, u32[]{:S(2)}, u32[]{:S(2)}) collective-permute-start(bf16[400,512]{1,0:T(8,128)(2,1)S(1)} %constant_dynamic-update-slice_fusion.3.mine), channel_id=1, source_target_pairs={{0,4},{1,5},{2,6},{3,7},{4,0},{5,1},{6,2},{7,3},{8,12},{9,13},{10,... | collective-permute-start | bytes 1228808 | tf_op jit(solution)/shard_map/ppermute | solution.py:38
  39.9 11.9 %collective-permute-start.14 = (bf16[400,512]{1,0:T(8,128)(2,1)S(1)}, bf16[400,512]{1,0:T(8,128)(2,1)S(1)}, u32[]{:S(2)}, u32[]{:S(2)}) collective-permute-start(bf16[400,512]{1,0:T(8,128)(2,1)S(1)} %constant_dynamic-update-slice_fusion.1.mine), channel_id=1, source_target_pairs={{0,1},{1,0},{2,3},{3,2},{4,5},{5,4},{6,7},{7,6},{8,9},{9,8},{10,11... | collective-permute-start | bytes 1228808 | tf_op jit(solution)/shard_map/ppermute | solution.py:38
  39.9 11.9 %collective-permute-start.9 = (bf16[400,512]{1,0:T(8,128)(2,1)S(1)}, bf16[400,512]{1,0:T(8,128)(2,1)S(1)}, u32[]{:S(2)}, u32[]{:S(2)}) collective-permute-start(bf16[400,512]{1,0:T(8,128)(2,1)S(1)} %constant_dynamic-update-slice_fusion.1.mine), channel_id=1, source_target_pairs={{0,2},{1,3},{2,0},{3,1},{4,6},{5,7},{6,4},{7,5},{8,10},{9,11},{10,... | collective-permute-start | bytes 1228808 | tf_op jit(solution)/shard_map/ppermute | solution.py:38
  41.4 4.0 %collective-permute-start.11 = (bf16[400,512]{1,0:T(8,128)(2,1)S(1)}, bf16[400,512]{1,0:T(8,128)(2,1)S(1)}, u32[]{:S(2)}, u32[]{:S(2)}) collective-permute-start(bf16[400,512]{1,0:T(8,128)(2,1)S(1)} %collective-permute-done.10.mine), channel_id=1, source_target_pairs={{0,1},{1,0},{2,3},{3,2},{4,5},{5,4},{6,7},{7,6},{8,9},{9,8},{10,11... | collective-permute-start | bytes 1228808 | tf_op jit(solution)/shard_map/ppermute | solution.py:38
  64.6 4.1 %collective-permute-start.16 = (bf16[384,512]{1,0:T(8,128)(2,1)S(1)}, bf16[384,512]{1,0:T(8,128)(2,1)S(1)}, u32[]{:S(2)}, u32[]{:S(2)}) collective-permute-start(bf16[384,512]{1,0:T(8,128)(2,1)S(1)} %get-tuple-element.104), channel_id=1, source_target_pairs={{0,1},{1,0},{2,3},{3,2},{4,5},{5,4},{6,7},{7,6},{8,9},{9,8},{10,11... | collective-permute-start | bytes 1179656 | tf_op jit(solution)/shard_map/ppermute | solution.py:38
  64.8 12.0 %collective-permute-start.19 = (bf16[384,512]{1,0:T(8,128)(2,1)S(1)}, bf16[384,512]{1,0:T(8,128)(2,1)S(1)}, u32[]{:S(2)}, u32[]{:S(2)}) collective-permute-start(bf16[384,512]{1,0:T(8,128)(2,1)S(1)} %add_convert_fusion.7.refs_0_), channel_id=1, source_target_pairs={{0,2},{1,3},{2,0},{3,1},{4,6},{5,7},{6,4},{7,5},{8,10},{9,11},{10,... | collective-permute-start | bytes 1179656 | tf_op jit(solution)/shard_map/ppermute | solution.py:38
  68.8 12.0 %collective-permute-start.21 = (bf16[384,512]{1,0:T(8,128)(2,1)S(1)}, bf16[384,512]{1,0:T(8,128)(2,1)S(1)}, u32[]{:S(2)}, u32[]{:S(2)}) collective-permute-start(bf16[384,512]{1,0:T(8,128)(2,1)S(1)} %add_convert_fusion.6.refs_0_), channel_id=1, source_target_pairs={{0,4},{1,5},{2,6},{3,7},{4,0},{5,1},{6,2},{7,3},{8,12},{9,13},{10,... | collective-permute-start | bytes 1179656 | tf_op jit(solution)/shard_map/ppermute | solution.py:38
  71.9 13.3 %collective-permute-start.23 = (bf16[384,512]{1,0:T(8,128)(2,1)S(1)}, bf16[384,512]{1,0:T(8,128)(2,1)S(1)}, u32[]{:S(2)}, u32[]{:S(2)}) collective-permute-start(bf16[384,512]{1,0:T(8,128)(2,1)S(1)} %add_convert_fusion.5.refs_0_), channel_id=1, source_target_pairs={{0,2},{1,3},{2,0},{3,1},{4,6},{5,7},{6,4},{7,5},{8,10},{9,11},{10,... | collective-permute-start | bytes 1179656 | tf_op jit(solution)/shard_map/ppermute | solution.py:38
  74.4 6.4 %collective-permute-start.20 = (bf16[384,512]{1,0:T(8,128)(2,1)S(1)}, bf16[384,512]{1,0:T(8,128)(2,1)S(1)}, u32[]{:S(2)}, u32[]{:S(2)}) collective-permute-start(bf16[384,512]{1,0:T(8,128)(2,1)S(1)} %get-tuple-element.113), channel_id=1, source_target_pairs={{0,1},{1,0},{2,3},{3,2},{4,5},{5,4},{6,7},{7,6},{8,9},{9,8},{10,11... | collective-permute-start | bytes 1179656 | tf_op jit(solution)/shard_map/ppermute | solution.py:38
  77.0 11.7 %collective-permute-start.24 = (bf16[384,512]{1,0:T(8,128)(2,1)S(1)}, bf16[384,512]{1,0:T(8,128)(2,1)S(1)}, u32[]{:S(2)}, u32[]{:S(2)}) collective-permute-start(bf16[384,512]{1,0:T(8,128)(2,1)S(1)} %add_convert_fusion.4.refs_0_), channel_id=1, source_target_pairs={{0,4},{1,5},{2,6},{3,7},{4,0},{5,1},{6,2},{7,3},{8,12},{9,13},{10,... | collective-permute-start | bytes 1179656 | tf_op jit(solution)/shard_map/ppermute | solution.py:38
  79.7 4.3 %collective-permute-start.22 = (bf16[384,512]{1,0:T(8,128)(2,1)S(1)}, bf16[384,512]{1,0:T(8,128)(2,1)S(1)}, u32[]{:S(2)}, u32[]{:S(2)}) collective-permute-start(bf16[384,512]{1,0:T(8,128)(2,1)S(1)} %get-tuple-element.116), channel_id=1, source_target_pairs={{0,1},{1,0},{2,3},{3,2},{4,5},{5,4},{6,7},{7,6},{8,9},{9,8},{10,11... | collective-permute-start | bytes 1179656 | tf_op jit(solution)/shard_map/ppermute | solution.py:38
  81.0 20.0 %collective-permute-start.28 = (bf16[384,512]{1,0:T(8,128)(2,1)S(1)}, bf16[384,512]{1,0:T(8,128)(2,1)S(1)}, u32[]{:S(2)}, u32[]{:S(2)}) collective-permute-start(bf16[384,512]{1,0:T(8,128)(2,1)S(1)} %add_convert_fusion.3.refs_0_), channel_id=1, source_target_pairs={{0,2},{1,3},{2,0},{3,1},{4,6},{5,7},{6,4},{7,5},{8,10},{9,11},{10,... | collective-permute-start | bytes 1179656 | tf_op jit(solution)/shard_map/ppermute | solution.py:38
  83.7 15.6 %collective-permute-start.26 = (bf16[384,512]{1,0:T(8,128)(2,1)S(1)}, bf16[384,512]{1,0:T(8,128)(2,1)S(1)}, u32[]{:S(2)}, u32[]{:S(2)}) collective-permute-start(bf16[384,512]{1,0:T(8,128)(2,1)S(1)} %get-tuple-element.120), channel_id=1, source_target_pairs={{0,1},{1,0},{2,3},{3,2},{4,5},{5,4},{6,7},{7,6},{8,9},{9,8},{10,11... | collective-permute-start | bytes 1179656 | tf_op jit(solution)/shard_map/ppermute | solution.py:38
  88.9 18.6 %collective-permute-start.29 = (bf16[384,512]{1,0:T(8,128)(2,1)S(1)}, bf16[384,512]{1,0:T(8,128)(2,1)S(1)}, u32[]{:S(2)}, u32[]{:S(2)}) collective-permute-start(bf16[384,512]{1,0:T(8,128)(2,1)S(1)} %add_convert_fusion.2.refs_0_), channel_id=1, source_target_pairs={{0,12},{1,13},{2,14},{3,15},{4,8},{5,9},{6,10},{7,11},{8,4},{9,5},... | collective-permute-start | bytes 1179656 | tf_op jit(solution)/shard_map/ppermute | solution.py:38
  99.4 14.5 %collective-permute-start.27 = (bf16[384,512]{1,0:T(8,128)(2,1)S(1)}, bf16[384,512]{1,0:T(8,128)(2,1)S(1)}, u32[]{:S(2)}, u32[]{:S(2)}) collective-permute-start(bf16[384,512]{1,0:T(8,128)(2,1)S(1)} %add_convert_fusion.1), channel_id=1, source_target_pairs={{0,4},{1,5},{2,6},{3,7},{4,0},{5,1},{6,2},{7,3},{8,12},{9,13},{10,... | collective-permute-start | bytes 1179656 | tf_op jit(solution)/shard_map/ppermute | solution.py:38
  (6 other events, 18.5 us)
